TPU v7x, 32 devices: a whole 2x2x4 slice. The times are simulated.
32 devices in a mesh: dp: 4 (over y, x), tensor: 8 (over z, core).
Axes of the slice: x: 2, y: 2, z: 4, core: 2. Of those that a mesh axis runs over, the one named last changes fastest.
Arguments:
- tokens_in: bfloat16 [4096, 8192], P('dp', 'tensor'), may hold values from -6 to 6
- out_grad: bfloat16 [4096, 8192], P('dp', 'tensor'), may hold values from -6 to 6
- left_up: bfloat16 [8192, 1024], P('tensor'), may hold values from -0.1875 to 0.1875
- right_up: bfloat16 [8192, 4096], P('tensor'), may hold values from -0.1875 to 0.1875
- left_down: bfloat16 [32768, 1024], P('tensor'), may hold values from -0.09375 to 0.09375
- right_down: bfloat16 [8192, 1024], P('tensor'), may hold values from -0.1875 to 0.1875
Outputs:
- layer_out: bfloat16 [4096, 8192], P('dp', 'tensor')
- input_grad: bfloat16 [4096, 8192], P('dp', 'tensor')
- grad_left_up: bfloat16 [8192, 1024], P('tensor')
- grad_right_up: bfloat16 [8192, 4096], P('tensor')
- grad_left_down: bfloat16 [32768, 1024], P('tensor')
- grad_right_down: bfloat16 [8192, 1024], P('tensor')
All inputs are finite; a program needn't handle non-finite values.
Results may differ from a plain program's by a relative error of at most 0.0075.
Values may be sent and summed in bfloat16 or wider, within the bound.
A program may use at most 192 MiB of HBM per device.

v0:
```python
import jax
import jax.numpy as jnp
from jax import lax
from jax.sharding import PartitionSpec as P


def gelu_tanh(values):
    return jax.nn.gelu(values, approximate=True)


def on_device(tokens_in, out_grad, left_up, right_up, left_down, right_down):
    blocks = lax.axis_size("tensor")
    tok_rows = tokens_in.shape[0]
    width = tokens_in.shape[1]
    sub_width = width // blocks
    hidden_width = right_up.shape[1]
    f32 = jnp.float32
    bf16 = jnp.bfloat16
    left_up_r = left_up.reshape(width, blocks, sub_width)
    right_up_r = right_up.reshape(blocks, sub_width, hidden_width)
    left_down_r = left_down.reshape(hidden_width, blocks, sub_width)
    right_down_r = right_down.reshape(blocks, sub_width, width)
    first = jnp.einsum("tk,kbs->bts", tokens_in, left_up_r, preferred_element_type=f32).astype(bf16)
    mixed_up = lax.all_to_all(
        first.reshape(blocks, tok_rows * sub_width),
        "tensor",
        split_axis=0,
        concat_axis=0,
        tiled=True,
    )
    mixed_up = mixed_up.reshape(blocks, tok_rows, sub_width)
    pre_act = jnp.einsum("bts,bsf->tf", mixed_up, right_up_r, preferred_element_type=f32)
    hidden = gelu_tanh(pre_act).astype(bf16)
    third = jnp.einsum("tf,fbs->bts", hidden, left_down_r, preferred_element_type=f32).astype(bf16)
    mixed_down = lax.all_to_all(
        third.reshape(blocks, tok_rows * sub_width),
        "tensor",
        split_axis=0,
        concat_axis=0,
        tiled=True,
    )
    mixed_down = mixed_down.reshape(blocks, tok_rows, sub_width)
    layer_out = jnp.einsum(
        "bts,bsk->tk", mixed_down, right_down_r, preferred_element_type=f32
    ).astype(bf16)
    part_right_down = jnp.einsum(
        "bts,tk->bsk", mixed_down, out_grad, preferred_element_type=f32
    ).reshape(width, width)
    back_mixed_down = jnp.einsum(
        "tk,bsk->bts", out_grad, right_down_r, preferred_element_type=f32
    ).astype(bf16)
    back_third = lax.all_to_all(
        back_mixed_down.reshape(blocks, tok_rows * sub_width),
        "tensor",
        split_axis=0,
        concat_axis=0,
        tiled=True,
    )
    back_third = back_third.reshape(blocks, tok_rows, sub_width)
    part_left_down = jnp.einsum(
        "tf,bts->fbs", hidden, back_third, preferred_element_type=f32
    ).reshape(hidden_width, width)
    back_hidden = jnp.einsum("bts,fbs->tf", back_third, left_down_r, preferred_element_type=f32)
    back_pre = jax.vjp(gelu_tanh, pre_act)[1](back_hidden)[0].astype(bf16)
    part_right_up = jnp.einsum(
        "bts,tf->bsf", mixed_up, back_pre, preferred_element_type=f32
    ).reshape(width, hidden_width)
    back_mixed_up = jnp.einsum(
        "tf,bsf->bts", back_pre, right_up_r, preferred_element_type=f32
    ).astype(bf16)
    back_first = lax.all_to_all(
        back_mixed_up.reshape(blocks, tok_rows * sub_width),
        "tensor",
        split_axis=0,
        concat_axis=0,
        tiled=True,
    )
    back_first = back_first.reshape(blocks, tok_rows, sub_width)
    part_left_up = jnp.einsum(
        "tk,bts->kbs", tokens_in, back_first, preferred_element_type=f32
    ).reshape(width, width)
    input_grad = jnp.einsum(
        "bts,kbs->tk", back_first, left_up_r, preferred_element_type=f32
    ).astype(bf16)
    part_left_up, part_right_up, part_left_down, part_right_down = lax.psum(
        (part_left_up, part_right_up, part_left_down, part_right_down), "dp"
    )
    return (
        layer_out,
        input_grad,
        part_left_up.astype(bf16),
        part_right_up.astype(bf16),
        part_left_down.astype(bf16),
        part_right_down.astype(bf16),
    )


def solution(mesh):
    return jax.shard_map(
        on_device,
        mesh=mesh,
        in_specs=(
            P("dp", "tensor"),
            P("dp", "tensor"),
            P("tensor", None),
            P("tensor", None),
            P("tensor", None),
            P("tensor", None),
        ),
        out_specs=(
            P("dp", "tensor"),
            P("dp", "tensor"),
            P("tensor", None),
            P("tensor", None),
            P("tensor", None),
            P("tensor", None),
        ),
        check_vma=False,
    )
```

profile of v0, /device:TPU:0, one launch (start us, length us, event | category | flops | bytes accessed | tf_op | source)
XLA Modules:
  0.0 1804.0 jit_solution(5524809870434454089)
XLA Ops:
  11.4 6.2 all_to_all.34
  18.2 14.3 reduce.6
  37.2 6.6 all-to-all-start.2
  59.9 14.3 reduce.4
  78.9 14.0 all-to-all-done.2
  97.5 6.8 reshape.91
  104.3 13.7 reduce.2
  118.0 28.6 %all-to-all-done = bf16[8,2,65536]{2,1,0:T(2,128)(2,1)} async-done(((bf16[8,2,65536]{2,1,0:T(2,128)(2,1)}), bf16[8,2,65536]{2,1,0:T(2,128)(2,1)}, u32[]{:S(2)}, u32[]{:S(2)}) %all-to-all-start) | async-done | bytes 2097184 | tf_op jit(solution)/shard_map/all_to_all | solution.py:24
  146.6 6.7 reshape.87
  153.3 13.7 reduce
  167.0 14.5 fusion.27
  181.5 17.0 convert_bitcast_fusion.2
  204.8 14.8 reduce.5
  228.6 24.8 %fusion.6 = bf16[1024,4096]{1,0:T(8,128)(2,1)} fusion(f32[1024,4096,1]{1,0,2:T(8,128)} %fusion.27, bf16[1,8,1024,128]{3,1,2,0:T(8,128)(2,1)} %bitcast.149, bf16[4096,1024]{1,0:T(8,128)(2,1)} %param.10), kind=kOutput, calls=%fused_computation.8 | convolution fusion | flops 8673820672 | bytes 35651584 | tf_op jit(solution)/shard_map/bts,fbs->tf/dot_general | solution.py:63
  260.6 14.8 convert_bitcast_fusion
  281.6 14.3 reduce.7
  306.0 19.4 %fusion.55 = f32[4096,1024]{1,0:T(8,128)} fusion(bf16[1024,1024]{1,0:T(8,128)(2,1)} %bitcast.158, f32[1024,4096,1]{1,0,2:T(8,128)} %fusion.27), kind=kOutput, calls=%fused_computation.55 | convolution fusion | flops 8627683328 | bytes 35651584 | tf_op jit(solution)/shard_map/tf,bts->fbs/dot_general | solution.py:60
  331.0 16.0 fusion.58
  346.9 6.7 reshape.89
  353.7 13.7 reduce.1
  374.5 6.7 reshape.93
  381.2 13.7 reduce.3
  409.3 6.5 fusion.59
  421.1 1382.4 %all-reduce.2 = (bf16[1024,1024]{1,0:T(8,128)(2,1)}, bf16[1024,4096]{1,0:T(8,128)(2,1)}, bf16[4096,1024]{1,0:T(8,128)(2,1)}, bf16[1024,1024]{1,0:T(8,128)(2,1)}) all-reduce(f32[1024,1024]{1,0:T(8,128)} %copy.55, f32[1024,4096]{1,0:T(8,128)} %fusion.58, f32[4096,1024]{1,0:T(8,128)} %fusion.55, ...), channel_id=1, replica_groups=mesh['dp'=4,'tensor'=8] {'dp'}, use_global_device_ids=true, to_apply=%region_0.0 | all-reduce | flops 10485760 | bytes 62914560 | tf_op jit(solution)/shard_map/psum | solution.py:85
  (37 shorter events, 112.6 us)
Async XLA Ops:
  0.6 1.6 copy-start
  37.2 55.7 %all-to-all-start.2 = ((bf16[8,2,65536]{2,1,0:T(2,128)(2,1)}), bf16[8,2,65536]{2,1,0:T(2,128)(2,1)}, u32[]{:S(2)}, u32[]{:S(2)}) async-start(bf16[8,2,65536]{2,1,0:T(2,128)(2,1)} %reshape.90), calls=%async_computation.2 | async-start | bytes 4194304 | tf_op jit(solution)/shard_map/all_to_all | solution.py:52
  92.9 53.7 %all-to-all-start = ((bf16[8,2,65536]{2,1,0:T(2,128)(2,1)}), bf16[8,2,65536]{2,1,0:T(2,128)(2,1)}, u32[]{:S(2)}, u32[]{:S(2)}) async-start(bf16[8,2,65536]{2,1,0:T(2,128)(2,1)} %reshape.86), calls=%async_computation | async-start | bytes 4194304 | tf_op jit(solution)/shard_map/all_to_all | solution.py:24
  224.3 76.4 %all-to-all-start.1 = ((bf16[8,2,65536]{2,1,0:T(2,128)(2,1)}), bf16[8,2,65536]{2,1,0:T(2,128)(2,1)}, u32[]{:S(2)}, u32[]{:S(2)}) async-start(bf16[8,2,65536]{2,1,0:T(2,128)(2,1)} %reshape.88), calls=%async_computation.1 | async-start | bytes 4194304 | tf_op jit(solution)/shard_map/all_to_all | solution.py:35
  300.7 73.8 %all-to-all-start.3 = ((bf16[8,2,65536]{2,1,0:T(2,128)(2,1)}), bf16[8,2,65536]{2,1,0:T(2,128)(2,1)}, u32[]{:S(2)}, u32[]{:S(2)}) async-start(bf16[8,2,65536]{2,1,0:T(2,128)(2,1)} %reshape.92), calls=%async_computation.3 | async-start | bytes 4194304 | tf_op jit(solution)/shard_map/all_to_all | solution.py:71
  306.0 19.5 %copy-start.1 = (bf16[8,131072]{1,0:T(8,128)(2,1)S(1)}, bf16[8,131072]{1,0:T(8,128)(2,1)}, u32[]{:S(2)}) copy-start(bf16[8,131072]{1,0:T(8,128)(2,1)} %reduce) | copy-start | bytes 6291460
  367.4 3.3 copy-start.2
  394.9 6.1 copy-start.3
  394.9 6.1 copy-start.4
where the time goes:
time: 1810 us; the launch traced here: 1800 us
  blocking collectives  1380 us (76%)
  matrix products  138 us (8%)
  other arithmetic  112 us (6%)
  local copies, waits for them, and re-layouts  106 us (6%)
  waiting for transfers between devices  42.6 us (2%)
  starting transfers between devices  20.8 us (1%)
    psum x1, blocking collectives, on_device(): lax.psum((part_left_up, part_right_up, part_left_down, part_right_down),...  1380 us
    unnamed x21, local copies, waits for them, and re-layouts  55.8 us
  transfers between devices with their start and end apart: 4, of which 2 were waited for; matrix products, arithmetic and copies ran while one was open for 10% of the time, Pallas kernels for 0%

commit v1 on v0

v1 whole, which is shorter than its diff:
```python
import jax
import jax.numpy as jnp
from jax import lax
from jax.sharding import PartitionSpec as P

F32 = jnp.float32
BF16 = jnp.bfloat16


def gelu_tanh(values):
    return jax.nn.gelu(values, approximate=True)


def dot(left, right, left_dim, right_dim):
    return lax.dot_general(
        left, right, (((left_dim,), (right_dim,)), ((), ())), preferred_element_type=F32
    )


def swap_blocks(values, blocks):
    tok_rows, width = values.shape
    sub = width // blocks
    parts = values.reshape(tok_rows, blocks, sub).transpose(1, 0, 2)
    parts = lax.all_to_all(parts, "tensor", split_axis=0, concat_axis=0, tiled=True)
    return parts.transpose(1, 0, 2).reshape(tok_rows, width)


def exchange(values, bit):
    size = lax.axis_size("dp")
    return lax.ppermute(values, "dp", [(i, i ^ (1 << bit)) for i in range(size)])


def start_sum(left, right, bits):
    me = lax.axis_index("dp")
    half = left.shape[1] // 2
    mine = (me >> bits[0]) & 1
    away = dot(lax.dynamic_slice_in_dim(left, (1 - mine) * half, half, 1), right, 0, 0).astype(BF16)
    got = exchange(away, bits[0])
    kept = dot(lax.dynamic_slice_in_dim(left, mine * half, half, 1), right, 0, 0)
    return kept + got.astype(F32)


def finish_sum(total, bits):
    me = lax.axis_index("dp")
    for bit in bits[1:]:
        half = total.shape[0] // 2
        mine = (me >> bit) & 1
        away = lax.dynamic_slice_in_dim(total, (1 - mine) * half, half, 0).astype(BF16)
        got = exchange(away, bit)
        total = lax.dynamic_slice_in_dim(total, mine * half, half, 0) + got.astype(F32)
    total = total.astype(BF16)
    for bit in reversed(bits):
        mine = (me >> bit) & 1
        got = exchange(total, bit)
        first = jnp.where(mine == 0, total, got)
        second = jnp.where(mine == 0, got, total)
        total = jnp.concatenate([first, second], axis=0)
    return total


def summed_product(left, right, pieces):
    size = lax.axis_size("dp")
    bits = list(range(size.bit_length() - 1))
    rows = left.shape[1] // pieces
    out = []
    for piece in range(pieces):
        order = bits if piece % 2 == 0 else bits[::-1]
        cut = lax.slice_in_dim(left, piece * rows, (piece + 1) * rows, axis=1)
        if order:
            out.append(finish_sum(start_sum(cut, right, order), order))
        else:
            out.append(dot(cut, right, 0, 0).astype(BF16))
    return jnp.concatenate(out, axis=0)


def on_device(tokens_in, out_grad, left_up, right_up, left_down, right_down):
    blocks = lax.axis_size("tensor")
    first = dot(tokens_in, left_up, 1, 0).astype(BF16)
    mixed_up = swap_blocks(first, blocks)
    back_mixed_down = dot(out_grad, right_down, 1, 1).astype(BF16)
    back_third = swap_blocks(back_mixed_down, blocks)

    pre_act = dot(mixed_up, right_up, 1, 0)
    hidden = gelu_tanh(pre_act).astype(BF16)
    grad_left_down = summed_product(hidden, back_third, 4)
    back_hidden = dot(back_third, left_down, 1, 1)
    back_pre = jax.vjp(gelu_tanh, pre_act)[1](back_hidden)[0].astype(BF16)
    grad_right_up = summed_product(mixed_up, back_pre, 4)
    third = dot(hidden, left_down, 1, 0).astype(BF16)
    mixed_down = swap_blocks(third, blocks)
    back_mixed_up = dot(back_pre, right_up, 1, 1).astype(BF16)
    back_first = swap_blocks(back_mixed_up, blocks)

    grad_right_down = summed_product(mixed_down, out_grad, 2)
    layer_out = dot(mixed_down, right_down, 1, 0).astype(BF16)
    grad_left_up = summed_product(tokens_in, back_first, 2)
    input_grad = dot(back_first, left_up, 1, 1).astype(BF16)
    return layer_out, input_grad, grad_left_up, grad_right_up, grad_left_down, grad_right_down


def solution(mesh):
    specs = (P("dp", "tensor"),) * 2 + (P("tensor", None),) * 4
    return jax.shard_map(on_device, mesh=mesh, in_specs=specs, out_specs=specs, check_vma=False)
```

time: 1810 us -> 652 us (0.36)
  blocking collectives: 1380 us -> 0 us
  waiting for transfers between devices: 42.6 us -> 358 us
  other arithmetic: 112 us -> 26.6 us
  local copies, waits for them, and re-layouts: 106 us -> 22.5 us
  starting transfers between devices: 20.8 us -> 82.5 us
    psum x1 -> x0, blocking collectives: 1380 us -> none  [on_device(): lax.psum((part_left_up, part_right_up, part_left_down, part_right_down),...]
    ppermute x0 -> x48, waiting for transfers between devices: none -> 236 us  [exchange(): return lax.ppermute(values, 'dp', [(i, i ^ 1 << bit) for i in range(size)])]
    all_to_all x8 -> x0, other arithmetic: 112 us -> none  [the longest x2 28.4 us: on_device(): lax.all_to_all(third.reshape(blocks, tok_rows * sub_width), 'tensor', spl...]
    all_to_all x4, waiting for transfers between devices: 42.6 us -> 122 us  [swap_blocks(): lax.all_to_all(parts, 'tensor', split_axis=0, concat_axis=0, tiled=True)]
    ppermute x0 -> x48, starting transfers between devices: none -> 61 us  [exchange(): return lax.ppermute(values, 'dp', [(i, i ^ 1 << bit) for i in range(size)])]
    unnamed x21 -> x44, local copies, waits for them, and re-layouts: 55.8 us -> 6.71 us
    all_to_all x5 -> x0, local copies, waits for them, and re-layouts: 25.5 us -> none  [the longest x2 6.75 us: on_device(): lax.all_to_all(first.reshape(blocks, tok_rows * sub_width), 'tensor', spl...]
    dot_general x12 -> x32, matrix products: 138 us -> 152 us  [dot(): lax.dot_general(left, right, (((left_dim,), (right_dim,)), ((), ())), pre...]
  transfers between devices with their start and end apart: 4 -> 52, of which waited for: 2 -> 30; matrix products, arithmetic and copies ran while one was open for 10% -> 14% of each run, Pallas kernels for 0% -> 0%
where the time goes in v1:
time: 652 us; the launch traced here: 643 us
  waiting for transfers between devices  358 us (55%)
  matrix products  152 us (23%)
  starting transfers between devices  82.5 us (13%)
  other arithmetic  26.6 us (4%)
  local copies, waits for them, and re-layouts  22.5 us (3%)
    ppermute x48, waiting for transfers between devices, exchange(): return lax.ppermute(values, 'dp', [(i, i ^ 1 << bit) for i in range(size)])  236 us
    dot_general x32, matrix products, dot(): lax.dot_general(left, right, (((left_dim,), (right_dim,)), ((), ())), pre...  152 us
    all_to_all x4, waiting for transfers between devices, swap_blocks(): lax.all_to_all(parts, 'tensor', split_axis=0, concat_axis=0, tiled=True)  122 us
    ppermute x48, starting transfers between devices, exchange(): return lax.ppermute(values, 'dp', [(i, i ^ 1 << bit) for i in range(size)])  61 us
    all_to_all x4, starting transfers between devices, swap_blocks(): lax.all_to_all(parts, 'tensor', split_axis=0, concat_axis=0, tiled=True)  21.5 us
    slice x4, local copies, waits for them, and re-layouts, summed_product(): cut = lax.slice_in_dim(left, piece * rows, (piece + 1) * rows, axis=1)  15.1 us
    unnamed x15, other arithmetic  15 us
  transfers between devices with their start and end apart: 52, of which 30 were waited for; matrix products, arithmetic and copies ran while one was open for 14% of the time, Pallas kernels for 0%

profile of v1, /device:TPU:0, one launch (start us, length us, event | category | flops | bytes accessed | tf_op | source)
XLA Modules:
  0.0 643.4 jit_solution(8619179774180664546)
XLA Ops:
  18.3 43.9 %all-to-all-done = bf16[8,1024,128]{1,2,0:T(8,128)(2,1)} async-done(((bf16[8,1024,128]{1,2,0:T(8,128)(2,1)}), bf16[8,1024,128]{1,2,0:T(8,128)(2,1)}, u32[]{:S(2)}, u32[]{:S(2)}) %all-to-all-start) | async-done | bytes 2097184 | tf_op jit(solution)/shard_map/all_to_all | solution.py:24
  72.4 43.2 %all-to-all-done.2 = bf16[8,1024,128]{1,2,0:T(8,128)(2,1)} async-done(((bf16[8,1024,128]{1,2,0:T(8,128)(2,1)}), bf16[8,1024,128]{1,2,0:T(8,128)(2,1)}, u32[]{:S(2)}, u32[]{:S(2)}) %all-to-all-start.2) | async-done | bytes 2097184 | tf_op jit(solution)/shard_map/all_to_all | solution.py:24
  115.6 16.2 %fusion.95 = f32[1024,4096]{1,0:T(8,128)} fusion(bf16[1024,1024]{0,1:T(8,128)(2,1)} %bitcast.11, bf16[4096,1024]{1,0:T(8,128)(2,1)} %param.10), kind=kOutput, calls=%fused_computation.190 | convolution fusion | flops 8589934592 | bytes 27262976 | tf_op jit(solution)/shard_map/dot_general | solution.py:15
  131.8 28.9 %fusion.6 = (bf16[1024,4096]{1,0:T(8,128)(2,1)}, bf16[1024,4096]{1,0:T(8,128)(2,1)}) fusion(f32[1024,4096]{1,0:T(8,128)} %fusion.95, bf16[1024,1024]{0,1:T(8,128)(2,1)} %bitcast.3, bf16[1024,4096]{1,0:T(8,128)(2,1)} %param.9), kind=kOutput, calls=%fused_computation.8 | convolution fusion | flops 8682209280 | bytes 44040192 | tf_op jit(solution)/shard_map/dot_general | solution.py:15
  160.7 15.1 %convolution_convert_fusion.5 = bf16[1024,1024]{0,1:T(8,128)(2,1)} fusion(bf16[1024,4096]{1,0:T(8,128)(2,1)} %get-tuple-element.7, bf16[4096,1024]{1,0:T(8,128)(2,1)} %param.10), kind=kOutput, calls=%fused_computation.25 | convolution fusion | flops 8590983168 | bytes 18874368 | tf_op jit(solution)/shard_map/dot_general | solution.py:15
  175.8 6.5 %fusion.91 = (bf16[1024,1024]{1,0:T(8,128)(2,1)}, bf16[1024,1024]{1,0:T(8,128)(2,1)}, bf16[1024,1024]{1,0:T(8,128)(2,1)}, bf16[1024,1024]{1,0:T(8,128)(2,1)}) fusion(bf16[1024,4096]{1,0:T(8,128)(2,1)} %get-tuple-element.7), kind=kLoop, calls=%fused_computation.186 | loop fusion | bytes 16777216 | tf_op jit(solution)/shard_map/slice | solution.py:68
  184.6 12.3 %convolution_convert_fusion.4 = bf16[1024,1024]{0,1:T(8,128)(2,1)} fusion(bf16[1024,4096]{1,0:T(8,128)(2,1)S(1)} %copy-done.1, bf16[1024,4096]{1,0:T(8,128)(2,1)} %param.9), kind=kOutput, calls=%fused_computation.24 | convolution fusion | flops 8590983168 | bytes 18874368 | tf_op jit(solution)/shard_map/dot_general | solution.py:15
  236.6 18.4 %collective-permute-done.16 = bf16[128,4096]{1,0:T(8,128)(2,1)} collective-permute-done((bf16[128,4096]{1,0:T(8,128)(2,1)}, bf16[128,4096]{1,0:T(8,128)(2,1)}, u32[]{:S(2)}, u32[]{:S(2)}) %collective-permute-start.16) | collective-permute-done | bytes 1048608 | tf_op jit(solution)/shard_map/ppermute | solution.py:30
  262.5 14.9 %collective-permute-done.24 = bf16[512,1024]{1,0:T(8,128)(2,1)S(1)} collective-permute-done((bf16[512,1024]{1,0:T(8,128)(2,1)S(1)}, bf16[512,1024]{1,0:T(8,128)(2,1)S(1)}, u32[]{:S(2)}, u32[]{:S(2)}) %collective-permute-start.24) | collective-permute-done | bytes 1048608 | tf_op jit(solution)/shard_map/ppermute | solution.py:30
  286.5 13.3 %collective-permute-done.32 = bf16[512,1024]{1,0:T(8,128)(2,1)S(1)} collective-permute-done((bf16[512,1024]{1,0:T(8,128)(2,1)S(1)}, bf16[512,1024]{1,0:T(8,128)(2,1)S(1)}, u32[]{:S(2)}, u32[]{:S(2)}) %collective-permute-start.32) | collective-permute-done | bytes 1048608 | tf_op jit(solution)/shard_map/ppermute | solution.py:30
  316.4 9.6 %collective-permute-done.17 = bf16[64,4096]{1,0:T(8,128)(2,1)S(1)} collective-permute-done((bf16[64,4096]{1,0:T(8,128)(2,1)S(1)}, bf16[64,4096]{1,0:T(8,128)(2,1)S(1)}, u32[]{:S(2)}, u32[]{:S(2)}) %collective-permute-start.17) | collective-permute-done | bytes 524320 | tf_op jit(solution)/shard_map/ppermute | solution.py:30
  330.1 7.2 %collective-permute-done.25 = bf16[256,1024]{1,0:T(8,128)(2,1)S(1)} collective-permute-done((bf16[256,1024]{1,0:T(8,128)(2,1)S(1)}, bf16[256,1024]{1,0:T(8,128)(2,1)S(1)}, u32[]{:S(2)}, u32[]{:S(2)}) %collective-permute-start.25) | collective-permute-done | bytes 524320 | tf_op jit(solution)/shard_map/ppermute | solution.py:30
  338.9 9.6 %collective-permute-done.33 = bf16[256,1024]{1,0:T(8,128)(2,1)S(1)} collective-permute-done((bf16[256,1024]{1,0:T(8,128)(2,1)S(1)}, bf16[256,1024]{1,0:T(8,128)(2,1)S(1)}, u32[]{:S(2)}, u32[]{:S(2)}) %collective-permute-start.33) | collective-permute-done | bytes 524320 | tf_op jit(solution)/shard_map/ppermute | solution.py:30
  361.3 9.6 %collective-permute-done.18 = bf16[64,4096]{1,0:T(8,128)(2,1)S(1)} collective-permute-done((bf16[64,4096]{1,0:T(8,128)(2,1)S(1)}, bf16[64,4096]{1,0:T(8,128)(2,1)S(1)}, u32[]{:S(2)}, u32[]{:S(2)}) %collective-permute-start.18) | collective-permute-done | bytes 524320 | tf_op jit(solution)/shard_map/ppermute | solution.py:30
  375.2 7.0 %collective-permute-done.26 = bf16[256,1024]{1,0:T(8,128)(2,1)S(1)} collective-permute-done((bf16[256,1024]{1,0:T(8,128)(2,1)S(1)}, bf16[256,1024]{1,0:T(8,128)(2,1)S(1)}, u32[]{:S(2)}, u32[]{:S(2)}) %collective-permute-start.26) | collective-permute-done | bytes 524320 | tf_op jit(solution)/shard_map/ppermute | solution.py:30
  383.9 9.5 %collective-permute-done.34 = bf16[256,1024]{1,0:T(8,128)(2,1)S(1)} collective-permute-done((bf16[256,1024]{1,0:T(8,128)(2,1)S(1)}, bf16[256,1024]{1,0:T(8,128)(2,1)S(1)}, u32[]{:S(2)}, u32[]{:S(2)}) %collective-permute-start.34) | collective-permute-done | bytes 524320 | tf_op jit(solution)/shard_map/ppermute | solution.py:30
  399.8 57.9 %collective-permute-done.27 = bf16[512,1024]{1,0:T(8,128)(2,1)S(1)} collective-permute-done((bf16[512,1024]{1,0:T(8,128)(2,1)S(1)}, bf16[512,1024]{1,0:T(8,128)(2,1)S(1)}, u32[]{:S(2)}, u32[]{:S(2)}) %collective-permute-start.27) | collective-permute-done | bytes 1048608 | tf_op jit(solution)/shard_map/ppermute | solution.py:30
  467.7 11.0 %collective-permute-done.35 = bf16[512,1024]{1,0:T(8,128)(2,1)S(1)} collective-permute-done((bf16[512,1024]{1,0:T(8,128)(2,1)S(1)}, bf16[512,1024]{1,0:T(8,128)(2,1)S(1)}, u32[]{:S(2)}, u32[]{:S(2)}) %collective-permute-start.35) | collective-permute-done | bytes 1048608 | tf_op jit(solution)/shard_map/ppermute | solution.py:30
  482.0 13.8 %collective-permute-done.39 = bf16[512,1024]{1,0:T(8,128)(2,1)S(1)} collective-permute-done((bf16[512,1024]{1,0:T(8,128)(2,1)S(1)}, bf16[512,1024]{1,0:T(8,128)(2,1)S(1)}, u32[]{:S(2)}, u32[]{:S(2)}) %collective-permute-start.39) | collective-permute-done | bytes 1048608 | tf_op jit(solution)/shard_map/ppermute | solution.py:30
  503.7 6.3 all-to-all-start.3
  524.2 34.9 %all-to-all-done.3 = bf16[8,1024,128]{1,2,0:T(8,128)(2,1)} async-done(((bf16[8,1024,128]{1,2,0:T(8,128)(2,1)}), bf16[8,1024,128]{1,2,0:T(8,128)(2,1)}, u32[]{:S(2)}, u32[]{:S(2)}) %all-to-all-start.3) | async-done | bytes 2097184 | tf_op jit(solution)/shard_map/all_to_all | solution.py:24
  575.8 9.2 %collective-permute-done = bf16[256,1024]{1,0:T(8,128)(2,1)S(1)} collective-permute-done((bf16[256,1024]{1,0:T(8,128)(2,1)S(1)}, bf16[256,1024]{1,0:T(8,128)(2,1)S(1)}, u32[]{:S(2)}, u32[]{:S(2)}) %collective-permute-start) | collective-permute-done | bytes 524320 | tf_op jit(solution)/shard_map/ppermute | solution.py:30
  622.2 9.1 %collective-permute-done.3 = bf16[256,1024]{1,0:T(8,128)(2,1)S(1)} collective-permute-done((bf16[256,1024]{1,0:T(8,128)(2,1)S(1)}, bf16[256,1024]{1,0:T(8,128)(2,1)S(1)}, u32[]{:S(2)}, u32[]{:S(2)}) %collective-permute-start.3) | collective-permute-done | bytes 524320 | tf_op jit(solution)/shard_map/ppermute | solution.py:30
  633.5 7.6 %collective-permute-done.47 = bf16[256,1024]{1,0:T(8,128)(2,1)S(1)} collective-permute-done((bf16[256,1024]{1,0:T(8,128)(2,1)S(1)}, bf16[256,1024]{1,0:T(8,128)(2,1)S(1)}, u32[]{:S(2)}, u32[]{:S(2)}) %collective-permute-start.47) | collective-permute-done | bytes 524320 | tf_op jit(solution)/shard_map/ppermute | solution.py:30
  (231 shorter events, 226.4 us)
Async XLA Ops:
  6.7 55.5 %all-to-all-start = ((bf16[8,1024,128]{1,2,0:T(8,128)(2,1)}), bf16[8,1024,128]{1,2,0:T(8,128)(2,1)}, u32[]{:S(2)}, u32[]{:S(2)}) async-start(bf16[8,1024,128]{1,2,0:T(8,128)(2,1)} %bitcast.69), calls=%async_computation | async-start | bytes 4194304 | tf_op jit(solution)/shard_map/all_to_all | solution.py:24
  62.2 53.4 %all-to-all-start.2 = ((bf16[8,1024,128]{1,2,0:T(8,128)(2,1)}), bf16[8,1024,128]{1,2,0:T(8,128)(2,1)}, u32[]{:S(2)}, u32[]{:S(2)}) async-start(bf16[8,1024,128]{1,2,0:T(8,128)(2,1)} %bitcast.68), calls=%async_computation.2 | async-start | bytes 4194304 | tf_op jit(solution)/shard_map/all_to_all | solution.py:24
  207.6 51.5 %collective-permute-start.12 = (bf16[128,4096]{1,0:T(8,128)(2,1)}, bf16[128,4096]{1,0:T(8,128)(2,1)}, u32[]{:S(2)}, u32[]{:S(2)}) collective-permute-start(bf16[128,4096]{1,0:T(8,128)(2,1)} %convolution_convert_fusion.2), channel_id=1, source_target_pairs={{0,16},{8,24},{16,0},{24,8},{1,17},{9,25},{17,1},{25,9},{2,18},{10... | collective-permute-start | bytes 3145736 | tf_op jit(solution)/shard_map/ppermute | solution.py:30
  209.1 45.8 %collective-permute-start.16 = (bf16[128,4096]{1,0:T(8,128)(2,1)}, bf16[128,4096]{1,0:T(8,128)(2,1)}, u32[]{:S(2)}, u32[]{:S(2)}) collective-permute-start(bf16[128,4096]{1,0:T(8,128)(2,1)} %convolution_convert_fusion.1), channel_id=1, source_target_pairs={{0,8},{8,0},{16,24},{24,16},{1,9},{9,1},{17,25},{25,17},{2,10},{10... | collective-permute-start | bytes 3145736 | tf_op jit(solution)/shard_map/ppermute | solution.py:30
  209.7 72.1 %collective-permute-start.20 = (bf16[128,4096]{1,0:T(8,128)(2,1)}, bf16[128,4096]{1,0:T(8,128)(2,1)}, u32[]{:S(2)}, u32[]{:S(2)}) collective-permute-start(bf16[128,4096]{1,0:T(8,128)(2,1)} %convolution_convert_fusion), channel_id=1, source_target_pairs={{0,16},{8,24},{16,0},{24,8},{1,17},{9,25},{17,1},{25,9},{2,18},{10... | collective-permute-start | bytes 3145736 | tf_op jit(solution)/shard_map/ppermute | solution.py:30
  210.2 293.5 %all-to-all-start.1 = ((bf16[8,1024,128]{1,2,0:T(8,128)(2,1)}), bf16[8,1024,128]{1,2,0:T(8,128)(2,1)}, u32[]{:S(2)}, u32[]{:S(2)}) async-start(bf16[8,1024,128]{1,2,0:T(8,128)(2,1)} %bitcast.67), calls=%async_computation.1 | async-start | bytes 4194304 | tf_op jit(solution)/shard_map/all_to_all | solution.py:24
  224.3 53.0 %collective-permute-start.24 = (bf16[512,1024]{1,0:T(8,128)(2,1)S(1)}, bf16[512,1024]{1,0:T(8,128)(2,1)S(1)}, u32[]{:S(2)}, u32[]{:S(2)}) collective-permute-start(bf16[512,1024]{1,0:T(8,128)(2,1)S(1)} %convolution_convert_fusion.13), channel_id=1, source_target_pairs={{0,8},{8,0},{16,24},{24,16},{1,9},{9,1},{17,25},{25,17},{2,10},{10... | collective-permute-start | bytes 3145736 | tf_op jit(solution)/shard_map/ppermute | solution.py:30
  232.5 67.3 %collective-permute-start.32 = (bf16[512,1024]{1,0:T(8,128)(2,1)S(1)}, bf16[512,1024]{1,0:T(8,128)(2,1)S(1)}, u32[]{:S(2)}, u32[]{:S(2)}) collective-permute-start(bf16[512,1024]{1,0:T(8,128)(2,1)S(1)} %convolution_convert_fusion.11), channel_id=1, source_target_pairs={{0,8},{8,0},{16,24},{24,16},{1,9},{9,1},{17,25},{25,17},{2,10},{10... | collective-permute-start | bytes 3145736 | tf_op jit(solution)/shard_map/ppermute | solution.py:30
  255.0 49.5 %collective-permute-start.28 = (bf16[512,1024]{1,0:T(8,128)(2,1)S(1)}, bf16[512,1024]{1,0:T(8,128)(2,1)S(1)}, u32[]{:S(2)}, u32[]{:S(2)}) collective-permute-start(bf16[512,1024]{1,0:T(8,128)(2,1)S(1)} %convolution_convert_fusion.12), channel_id=1, source_target_pairs={{0,16},{8,24},{16,0},{24,8},{1,17},{9,25},{17,1},{25,9},{2,18},{10... | collective-permute-start | bytes 3145736 | tf_op jit(solution)/shard_map/ppermute | solution.py:30
  259.1 49.9 %collective-permute-start.36 = (bf16[512,1024]{1,0:T(8,128)(2,1)S(1)}, bf16[512,1024]{1,0:T(8,128)(2,1)S(1)}, u32[]{:S(2)}, u32[]{:S(2)}) collective-permute-start(bf16[512,1024]{1,0:T(8,128)(2,1)S(1)} %convolution_convert_fusion.10), channel_id=1, source_target_pairs={{0,16},{8,24},{16,0},{24,8},{1,17},{9,25},{17,1},{25,9},{2,18},{10... | collective-permute-start | bytes 3145736 | tf_op jit(solution)/shard_map/ppermute | solution.py:30
  277.3 37.4 %collective-permute-start.9 = (bf16[64,4096]{1,0:T(8,128)(2,1)S(1)}, bf16[64,4096]{1,0:T(8,128)(2,1)S(1)}, u32[]{:S(2)}, u32[]{:S(2)}) collective-permute-start(bf16[64,4096]{1,0:T(8,128)(2,1)S(1)} %dynamic-slice_convert_fusion.7), channel_id=1, source_target_pairs={{0,16},{8,24},{16,0},{24,8},{1,17},{9,25},{17,1},{25,9},{2,18},{10... | collective-permute-start | bytes 1572872 | tf_op jit(solution)/shard_map/ppermute | solution.py:30
  281.8 45.8 %collective-permute-start.13 = (bf16[64,4096]{1,0:T(8,128)(2,1)S(1)}, bf16[64,4096]{1,0:T(8,128)(2,1)S(1)}, u32[]{:S(2)}, u32[]{:S(2)}) collective-permute-start(bf16[64,4096]{1,0:T(8,128)(2,1)S(1)} %dynamic-slice_convert_fusion.6), channel_id=1, source_target_pairs={{0,8},{8,0},{16,24},{24,16},{1,9},{9,1},{17,25},{25,17},{2,10},{10... | collective-permute-start | bytes 1572872 | tf_op jit(solution)/shard_map/ppermute | solution.py:30
  314.8 33.7 %collective-permute-start.33 = (bf16[256,1024]{1,0:T(8,128)(2,1)S(1)}, bf16[256,1024]{1,0:T(8,128)(2,1)S(1)}, u32[]{:S(2)}, u32[]{:S(2)}) collective-permute-start(bf16[256,1024]{1,0:T(8,128)(2,1)S(1)} %dynamic-slice_convert_fusion.1), channel_id=1, source_target_pairs={{0,16},{8,24},{16,0},{24,8},{1,17},{9,25},{17,1},{25,9},{2,18},{10... | collective-permute-start | bytes 1572872 | tf_op jit(solution)/shard_map/ppermute | solution.py:30
  328.3 31.4 %collective-permute-start.10 = (bf16[64,4096]{1,0:T(8,128)(2,1)S(1)}, bf16[64,4096]{1,0:T(8,128)(2,1)S(1)}, u32[]{:S(2)}, u32[]{:S(2)}) collective-permute-start(bf16[64,4096]{1,0:T(8,128)(2,1)S(1)} %add_convert_fusion.7), channel_id=1, source_target_pairs={{0,16},{8,24},{16,0},{24,8},{1,17},{9,25},{17,1},{25,9},{2,18},{10... | collective-permute-start | bytes 1572872 | tf_op jit(solution)/shard_map/ppermute | solution.py:30
  337.2 35.3 %collective-permute-start.14 = (bf16[64,4096]{1,0:T(8,128)(2,1)S(1)}, bf16[64,4096]{1,0:T(8,128)(2,1)S(1)}, u32[]{:S(2)}, u32[]{:S(2)}) collective-permute-start(bf16[64,4096]{1,0:T(8,128)(2,1)S(1)} %add_convert_fusion.6), channel_id=1, source_target_pairs={{0,8},{8,0},{16,24},{24,16},{1,9},{9,1},{17,25},{25,17},{2,10},{10... | collective-permute-start | bytes 1572872 | tf_op jit(solution)/shard_map/ppermute | solution.py:30
  352.1 30.1 %collective-permute-start.26 = (bf16[256,1024]{1,0:T(8,128)(2,1)S(1)}, bf16[256,1024]{1,0:T(8,128)(2,1)S(1)}, u32[]{:S(2)}, u32[]{:S(2)}) collective-permute-start(bf16[256,1024]{1,0:T(8,128)(2,1)S(1)} %add_convert_fusion.3), channel_id=1, source_target_pairs={{0,16},{8,24},{16,0},{24,8},{1,17},{9,25},{17,1},{25,9},{2,18},{10... | collective-permute-start | bytes 1572872 | tf_op jit(solution)/shard_map/ppermute | solution.py:30
  359.7 33.7 %collective-permute-start.34 = (bf16[256,1024]{1,0:T(8,128)(2,1)S(1)}, bf16[256,1024]{1,0:T(8,128)(2,1)S(1)}, u32[]{:S(2)}, u32[]{:S(2)}) collective-permute-start(bf16[256,1024]{1,0:T(8,128)(2,1)S(1)} %add_convert_fusion.1), channel_id=1, source_target_pairs={{0,16},{8,24},{16,0},{24,8},{1,17},{9,25},{17,1},{25,9},{2,18},{10... | collective-permute-start | bytes 1572872 | tf_op jit(solution)/shard_map/ppermute | solution.py:30
  373.3 94.1 %collective-permute-start.11 = (bf16[128,4096]{1,0:T(8,128)(2,1)S(1)}, bf16[128,4096]{1,0:T(8,128)(2,1)S(1)}, u32[]{:S(2)}, u32[]{:S(2)}) collective-permute-start(bf16[128,4096]{1,0:T(8,128)(2,1)S(1)} %pad_maximum_fusion.2), channel_id=1, source_target_pairs={{0,8},{8,0},{16,24},{24,16},{1,9},{9,1},{17,25},{25,17},{2,10},{10... | collective-permute-start | bytes 3145736 | tf_op jit(solution)/shard_map/ppermute | solution.py:30
  382.2 99.5 %collective-permute-start.15 = (bf16[128,4096]{1,0:T(8,128)(2,1)S(1)}, bf16[128,4096]{1,0:T(8,128)(2,1)S(1)}, u32[]{:S(2)}, u32[]{:S(2)}) collective-permute-start(bf16[128,4096]{1,0:T(8,128)(2,1)S(1)} %pad_maximum_fusion.3), channel_id=1, source_target_pairs={{0,16},{8,24},{16,0},{24,8},{1,17},{9,25},{17,1},{25,9},{2,18},{10... | collective-permute-start | bytes 3145736 | tf_op jit(solution)/shard_map/ppermute | solution.py:30
  393.4 104.2 %collective-permute-start.19 = (bf16[128,4096]{1,0:T(8,128)(2,1)S(1)}, bf16[128,4096]{1,0:T(8,128)(2,1)S(1)}, u32[]{:S(2)}, u32[]{:S(2)}) collective-permute-start(bf16[128,4096]{1,0:T(8,128)(2,1)S(1)} %pad_maximum_fusion.4), channel_id=1, source_target_pairs={{0,8},{8,0},{16,24},{24,16},{1,9},{9,1},{17,25},{25,17},{2,10},{10... | collective-permute-start | bytes 3145736 | tf_op jit(solution)/shard_map/ppermute | solution.py:30
  395.0 62.7 %collective-permute-start.27 = (bf16[512,1024]{1,0:T(8,128)(2,1)S(1)}, bf16[512,1024]{1,0:T(8,128)(2,1)S(1)}, u32[]{:S(2)}, u32[]{:S(2)}) collective-permute-start(bf16[512,1024]{1,0:T(8,128)(2,1)S(1)} %pad_maximum_fusion.6), channel_id=1, source_target_pairs={{0,8},{8,0},{16,24},{24,16},{1,9},{9,1},{17,25},{25,17},{2,10},{10... | collective-permute-start | bytes 3145736 | tf_op jit(solution)/shard_map/ppermute | solution.py:30
  397.1 65.9 %collective-permute-start.31 = (bf16[512,1024]{1,0:T(8,128)(2,1)S(1)}, bf16[512,1024]{1,0:T(8,128)(2,1)S(1)}, u32[]{:S(2)}, u32[]{:S(2)}) collective-permute-start(bf16[512,1024]{1,0:T(8,128)(2,1)S(1)} %pad_maximum_fusion.7), channel_id=1, source_target_pairs={{0,16},{8,24},{16,0},{24,8},{1,17},{9,25},{17,1},{25,9},{2,18},{10... | collective-permute-start | bytes 3145736 | tf_op jit(solution)/shard_map/ppermute | solution.py:30
  457.7 54.9 %collective-permute-start.23 = (bf16[128,4096]{1,0:T(8,128)(2,1)}, bf16[128,4096]{1,0:T(8,128)(2,1)}, u32[]{:S(2)}, u32[]{:S(2)}) collective-permute-start(bf16[128,4096]{1,0:T(8,128)(2,1)} %pad_maximum_fusion.5), channel_id=1, source_target_pairs={{0,16},{8,24},{16,0},{24,8},{1,17},{9,25},{17,1},{25,9},{2,18},{10... | collective-permute-start | bytes 3145736 | tf_op jit(solution)/shard_map/ppermute | solution.py:30
  503.7 55.5 %all-to-all-start.3 = ((bf16[8,1024,128]{1,2,0:T(8,128)(2,1)}), bf16[8,1024,128]{1,2,0:T(8,128)(2,1)}, u32[]{:S(2)}, u32[]{:S(2)}) async-start(bf16[8,1024,128]{1,2,0:T(8,128)(2,1)} %bitcast.66), calls=%async_computation.3 | async-start | bytes 4194304 | tf_op jit(solution)/shard_map/all_to_all | solution.py:24
  (50 other events, 713.6 us)

commit v2 on v1

--- a/solution.py
+++ b/solution.py
@@ -1,6 +1,7 @@
 import jax
 import jax.numpy as jnp
 from jax import lax
+from jax.experimental import pallas as pl
 from jax.sharding import PartitionSpec as P
 
 F32 = jnp.float32
@@ -15,6 +16,21 @@
     return lax.dot_general(
         left, right, (((left_dim,), (right_dim,)), ((), ())), preferred_element_type=F32
     )
+
+
+def nothing(*refs):
+    pass
+
+
+def after(values, *earlier):
+    anywhere = pl.BlockSpec(memory_space=pl.ANY)
+    return pl.pallas_call(
+        nothing,
+        out_shape=jax.ShapeDtypeStruct(values.shape, values.dtype),
+        in_specs=[anywhere] * (1 + len(earlier)),
+        out_specs=anywhere,
+        input_output_aliases={0: 0},
+    )(values, *earlier)
 
 
 def swap_blocks(values, blocks):
@@ -40,7 +56,7 @@
     return kept + got.astype(F32)
 
 
-def finish_sum(total, bits):
+def scatter_sum(total, bits):
     me = lax.axis_index("dp")
     for bit in bits[1:]:
         half = total.shape[0] // 2
@@ -48,7 +64,11 @@
         away = lax.dynamic_slice_in_dim(total, (1 - mine) * half, half, 0).astype(BF16)
         got = exchange(away, bit)
         total = lax.dynamic_slice_in_dim(total, mine * half, half, 0) + got.astype(F32)
-    total = total.astype(BF16)
+    return total.astype(BF16)
+
+
+def gather_sum(total, bits):
+    me = lax.axis_index("dp")
     for bit in reversed(bits):
         mine = (me >> bit) & 1
         got = exchange(total, bit)
@@ -58,19 +78,26 @@
     return total
 
 
-def summed_product(left, right, pieces):
-    size = lax.axis_size("dp")
-    bits = list(range(size.bit_length() - 1))
+def piece_orders(pieces):
+    bits = list(range(lax.axis_size("dp").bit_length() - 1))
+    return [bits if piece % 2 == 0 else bits[::-1] for piece in range(pieces)]
+
+
+def reduced_product(left, right, pieces):
     rows = left.shape[1] // pieces
     out = []
-    for piece in range(pieces):
-        order = bits if piece % 2 == 0 else bits[::-1]
+    for piece, order in enumerate(piece_orders(pieces)):
         cut = lax.slice_in_dim(left, piece * rows, (piece + 1) * rows, axis=1)
         if order:
-            out.append(finish_sum(start_sum(cut, right, order), order))
+            out.append(scatter_sum(start_sum(cut, right, order), order))
         else:
             out.append(dot(cut, right, 0, 0).astype(BF16))
-    return jnp.concatenate(out, axis=0)
+    return out
+
+
+def gathered(shares):
+    orders = piece_orders(len(shares))
+    return jnp.concatenate([gather_sum(share, order) for share, order in zip(shares, orders)], axis=0)
 
 
 def on_device(tokens_in, out_grad, left_up, right_up, left_down, right_down):
@@ -82,20 +109,31 @@
 
     pre_act = dot(mixed_up, right_up, 1, 0)
     hidden = gelu_tanh(pre_act).astype(BF16)
-    grad_left_down = summed_product(hidden, back_third, 4)
+    third = dot(hidden, left_down, 1, 0).astype(BF16)
+    back_third = after(back_third, third)
+    mixed_down = swap_blocks(third, blocks)
+
+    share_left_down = reduced_product(hidden, back_third, 4)
     back_hidden = dot(back_third, left_down, 1, 1)
     back_pre = jax.vjp(gelu_tanh, pre_act)[1](back_hidden)[0].astype(BF16)
-    grad_right_up = summed_product(mixed_up, back_pre, 4)
-    third = dot(hidden, left_down, 1, 0).astype(BF16)
-    mixed_down = swap_blocks(third, blocks)
+    back_pre = after(back_pre, mixed_down)
     back_mixed_up = dot(back_pre, right_up, 1, 1).astype(BF16)
     back_first = swap_blocks(back_mixed_up, blocks)
+    share_right_up = reduced_product(mixed_up, back_pre, 4)
+    share_right_down = reduced_product(mixed_down, out_grad, 2)
+    share_left_up = reduced_product(tokens_in, back_first, 2)
+    share_left_down = [after(share, back_first) for share in share_left_down]
 
-    grad_right_down = summed_product(mixed_down, out_grad, 2)
     layer_out = dot(mixed_down, right_down, 1, 0).astype(BF16)
-    grad_left_up = summed_product(tokens_in, back_first, 2)
     input_grad = dot(back_first, left_up, 1, 1).astype(BF16)
-    return layer_out, input_grad, grad_left_up, grad_right_up, grad_left_down, grad_right_down
+    return (
+        layer_out,
+        input_grad,
+        gathered(share_left_up),
+        gathered(share_right_up),
+        gathered(share_left_down),
+        gathered(share_right_down),
+    )
 
 
 def solution(mesh):

time: 652 us -> 575 us (0.88)
  waiting for transfers between devices: 358 us -> 295 us
  starting transfers between devices: 82.5 us -> 70.1 us
  local copies, waits for them, and re-layouts: 22.5 us -> 31.3 us
  matrix products: 152 us -> 145 us
    all_to_all x4, waiting for transfers between devices: 122 us -> 49.3 us  [swap_blocks(): lax.all_to_all(parts, 'tensor', split_axis=0, concat_axis=0, tiled=True)]
    reshape x0 -> x5, local copies, waits for them, and re-layouts: none -> 16.1 us  [the longest x3 8.34 us: swap_blocks(): return parts.transpose(1, 0, 2).reshape(tok_rows, width)]
    ppermute x48, starting transfers between devices: 61 us -> 49.6 us  [exchange(): return lax.ppermute(values, 'dp', [(i, i ^ 1 << bit) for i in range(size)])]
    ppermute x48, waiting for transfers between devices: 236 us -> 246 us  [exchange(): return lax.ppermute(values, 'dp', [(i, i ^ 1 << bit) for i in range(size)])]
    dot_general x32, matrix products: 152 us -> 145 us  [dot(): lax.dot_general(left, right, (((left_dim,), (right_dim,)), ((), ())), pre...]
    unnamed x15 -> x16, other arithmetic: 15 us -> 11.4 us
  transfers between devices with their start and end apart: 52 -> 52, of which waited for: 30 -> 27; matrix products, arithmetic and copies ran while one was open for 14% -> 31% of each run, Pallas kernels for 0% -> 0%
where the time goes in v2:
time: 575 us; the launch traced here: 569 us
  waiting for transfers between devices  295 us (51%)
  matrix products  145 us (25%)
  starting transfers between devices  70.1 us (12%)
  local copies, waits for them, and re-layouts  31.3 us (5%)
  other arithmetic  26.5 us (5%)
    ppermute x48, waiting for transfers between devices, exchange(): return lax.ppermute(values, 'dp', [(i, i ^ 1 << bit) for i in range(size)])  246 us
    dot_general x32, matrix products, dot(): lax.dot_general(left, right, (((left_dim,), (right_dim,)), ((), ())), pre...  145 us
    ppermute x48, starting transfers between devices, exchange(): return lax.ppermute(values, 'dp', [(i, i ^ 1 << bit) for i in range(size)])  49.6 us
    all_to_all x4, waiting for transfers between devices, swap_blocks(): lax.all_to_all(parts, 'tensor', split_axis=0, concat_axis=0, tiled=True)  49.3 us
    all_to_all x4, starting transfers between devices, swap_blocks(): lax.all_to_all(parts, 'tensor', split_axis=0, concat_axis=0, tiled=True)  20.5 us
  transfers between devices with their start and end apart: 52, of which 27 were waited for; matrix products, arithmetic and copies ran while one was open for 31% of the time, Pallas kernels for 0%

profile of v2, /device:TPU:0, one launch (start us, length us, event | category | flops | bytes accessed | tf_op | source)
XLA Modules:
  0.0 569.5 jit_solution(11076879478170303371)
XLA Ops:
  0.6 6.1 %convolution_convert_fusion.9 = bf16[1024,1024]{0,1:T(8,128)(2,1)} fusion(bf16[1024,1024]{1,0:T(8,128)(2,1)} %param.6, bf16[1024,1024]{1,0:T(8,128)(2,1)} %param.8), kind=kOutput, calls=%fused_computation.33 | convolution fusion | flops 2148532224 | bytes 6291456 | tf_op jit(solution)/shard_map/dot_general | solution.py:16
  6.7 6.3 %all-to-all-start = ((bf16[8,1024,128]{1,2,0:T(8,128)(2,1)}), bf16[8,1024,128]{1,2,0:T(8,128)(2,1)}, u32[]{:S(2)}, u32[]{:S(2)}) async-start(bf16[8,1024,128]{1,2,0:T(8,128)(2,1)} %bitcast.99), calls=%async_computation | async-start | bytes 4194304 | tf_op jit(solution)/shard_map/all_to_all | solution.py:40
  25.3 37.0 %all-to-all-done = bf16[8,1024,128]{1,2,0:T(8,128)(2,1)} async-done(((bf16[8,1024,128]{1,2,0:T(8,128)(2,1)}), bf16[8,1024,128]{1,2,0:T(8,128)(2,1)}, u32[]{:S(2)}, u32[]{:S(2)}) %all-to-all-start) | async-done | bytes 2097184 | tf_op jit(solution)/shard_map/all_to_all | solution.py:40
  66.8 20.2 %multiply_convert_fusion = (bf16[1024,4096]{1,0:T(8,128)(2,1)S(1)}, f32[1024,4096]{1,0:T(8,128)}) fusion(bf16[1024,1024]{0,1:T(8,128)(2,1)} %bitcast.3, bf16[1024,4096]{1,0:T(8,128)(2,1)} %param.9), kind=kOutput, calls=%fused_computation.9 | convolution fusion | flops 8627683328 | bytes 35651584 | tf_op jit(solution)/shard_map/dot_general | solution.py:16
  87.0 11.2 %convolution_convert_fusion.5.refs_1_ = bf16[1024,1024]{1,0:T(8,128)(2,1)S(1)} fusion(bf16[1024,4096]{1,0:T(8,128)(2,1)S(1)} %get-tuple-element.50, bf16[4096,1024]{1,0:T(8,128)(2,1)} %param.10), kind=kOutput, calls=%fused_computation.29 | convolution fusion | flops 8590983168 | bytes 18874368 | tf_op jit(solution)/shard_map/dot_general | solution.py:16
  103.6 12.3 %all-to-all-done.2 = bf16[8,1024,128]{2,1,0:T(8,128)(2,1)} async-done(((bf16[8,1024,128]{2,1,0:T(8,128)(2,1)}), bf16[8,1024,128]{2,1,0:T(8,128)(2,1)}, u32[]{:S(2)}, u32[]{:S(2)}) %all-to-all-start.2) | async-done | bytes 2097184 | tf_op jit(solution)/shard_map/all_to_all | solution.py:40
  123.7 25.2 %fusion.6.refs_0_ = bf16[1024,4096]{1,0:T(8,128)(2,1)} fusion(f32[1024,4096]{1,0:T(8,128)} %get-tuple-element.51, bf16[1024,1024]{1,0:T(8,128)(2,1)} %shard_map.109, bf16[4096,1024]{1,0:T(8,128)(2,1)} %param.10), kind=kOutput, calls=%fused_computation.8 | convolution fusion | flops 8673820672 | bytes 35651584 | tf_op jit(solution)/shard_map/dot_general | solution.py:16
  163.4 14.8 %collective-permute-done.24 = bf16[512,1024]{1,0:T(8,128)(2,1)S(1)} collective-permute-done((bf16[512,1024]{1,0:T(8,128)(2,1)S(1)}, bf16[512,1024]{1,0:T(8,128)(2,1)S(1)}, u32[]{:S(2)}, u32[]{:S(2)}) %collective-permute-start.24) | collective-permute-done | bytes 1048608 | tf_op jit(solution)/shard_map/ppermute | solution.py:46
  181.2 19.0 %collective-permute-done.32 = bf16[512,1024]{1,0:T(8,128)(2,1)S(1)} collective-permute-done((bf16[512,1024]{1,0:T(8,128)(2,1)S(1)}, bf16[512,1024]{1,0:T(8,128)(2,1)S(1)}, u32[]{:S(2)}, u32[]{:S(2)}) %collective-permute-start.32) | collective-permute-done | bytes 1048608 | tf_op jit(solution)/shard_map/ppermute | solution.py:46
  208.5 8.3 %collective-permute-done.25 = bf16[256,1024]{1,0:T(8,128)(2,1)S(1)} collective-permute-done((bf16[256,1024]{1,0:T(8,128)(2,1)S(1)}, bf16[256,1024]{1,0:T(8,128)(2,1)S(1)}, u32[]{:S(2)}, u32[]{:S(2)}) %collective-permute-start.25) | collective-permute-done | bytes 524320 | tf_op jit(solution)/shard_map/ppermute | solution.py:46
  217.8 9.2 %collective-permute-done.33 = bf16[256,1024]{1,0:T(8,128)(2,1)S(1)} collective-permute-done((bf16[256,1024]{1,0:T(8,128)(2,1)S(1)}, bf16[256,1024]{1,0:T(8,128)(2,1)S(1)}, u32[]{:S(2)}, u32[]{:S(2)}) %collective-permute-start.33) | collective-permute-done | bytes 524320 | tf_op jit(solution)/shard_map/ppermute | solution.py:46
  242.1 14.9 %convolution_convert_fusion.4 = bf16[1024,1024]{0,1:T(8,128)(2,1)} fusion(bf16[1024,4096]{1,0:T(8,128)(2,1)} %shard_map.110, bf16[1024,4096]{1,0:T(8,128)(2,1)} %param.9), kind=kOutput, calls=%fused_computation.28 | convolution fusion | flops 8590983168 | bytes 18874368 | tf_op jit(solution)/shard_map/dot_general | solution.py:16
  290.4 22.9 %collective-permute-done.45 = bf16[128,1024]{1,0:T(8,128)(2,1)S(1)} collective-permute-done((bf16[128,1024]{1,0:T(8,128)(2,1)S(1)}, bf16[128,1024]{1,0:T(8,128)(2,1)S(1)}, u32[]{:S(2)}, u32[]{:S(2)}) %collective-permute-start.45) | collective-permute-done | bytes 262176 | tf_op jit(solution)/shard_map/ppermute | solution.py:46
  325.1 16.0 %collective-permute-done.20 = bf16[128,4096]{1,0:T(8,128)(2,1)S(1)} collective-permute-done((bf16[128,4096]{1,0:T(8,128)(2,1)S(1)}, bf16[128,4096]{1,0:T(8,128)(2,1)S(1)}, u32[]{:S(2)}, u32[]{:S(2)}) %collective-permute-start.20) | collective-permute-done | bytes 1048608 | tf_op jit(solution)/shard_map/ppermute | solution.py:46
  347.4 10.5 %collective-permute-done.9 = bf16[64,4096]{1,0:T(8,128)(2,1)S(1)} collective-permute-done((bf16[64,4096]{1,0:T(8,128)(2,1)S(1)}, bf16[64,4096]{1,0:T(8,128)(2,1)S(1)}, u32[]{:S(2)}, u32[]{:S(2)}) %collective-permute-start.9) | collective-permute-done | bytes 524320 | tf_op jit(solution)/shard_map/ppermute | solution.py:46
  360.2 8.9 %collective-permute-done.17 = bf16[64,4096]{1,0:T(8,128)(2,1)S(1)} collective-permute-done((bf16[64,4096]{1,0:T(8,128)(2,1)S(1)}, bf16[64,4096]{1,0:T(8,128)(2,1)S(1)}, u32[]{:S(2)}, u32[]{:S(2)}) %collective-permute-start.17) | collective-permute-done | bytes 524320 | tf_op jit(solution)/shard_map/ppermute | solution.py:46
  371.7 8.7 %collective-permute-done.47 = bf16[256,1024]{1,0:T(8,128)(2,1)S(1)} collective-permute-done((bf16[256,1024]{1,0:T(8,128)(2,1)S(1)}, bf16[256,1024]{1,0:T(8,128)(2,1)S(1)}, u32[]{:S(2)}, u32[]{:S(2)}) %collective-permute-start.47) | collective-permute-done | bytes 524320 | tf_op jit(solution)/shard_map/ppermute | solution.py:46
  383.9 7.7 %collective-permute-done.10 = bf16[64,4096]{1,0:T(8,128)(2,1)S(1)} collective-permute-done((bf16[64,4096]{1,0:T(8,128)(2,1)S(1)}, bf16[64,4096]{1,0:T(8,128)(2,1)S(1)}, u32[]{:S(2)}, u32[]{:S(2)}) %collective-permute-start.10) | collective-permute-done | bytes 524320 | tf_op jit(solution)/shard_map/ppermute | solution.py:46
  394.2 8.7 %collective-permute-done.18 = bf16[64,4096]{1,0:T(8,128)(2,1)S(1)} collective-permute-done((bf16[64,4096]{1,0:T(8,128)(2,1)S(1)}, bf16[64,4096]{1,0:T(8,128)(2,1)S(1)}, u32[]{:S(2)}, u32[]{:S(2)}) %collective-permute-start.18) | collective-permute-done | bytes 524320 | tf_op jit(solution)/shard_map/ppermute | solution.py:46
  405.4 12.7 %collective-permute-done.11 = bf16[128,4096]{1,0:T(8,128)(2,1)S(1)} collective-permute-done((bf16[128,4096]{1,0:T(8,128)(2,1)S(1)}, bf16[128,4096]{1,0:T(8,128)(2,1)S(1)}, u32[]{:S(2)}, u32[]{:S(2)}) %collective-permute-start.11) | collective-permute-done | bytes 1048608 | tf_op jit(solution)/shard_map/ppermute | solution.py:46
  427.8 10.4 %collective-permute-done.19 = bf16[128,4096]{1,0:T(8,128)(2,1)S(1)} collective-permute-done((bf16[128,4096]{1,0:T(8,128)(2,1)S(1)}, bf16[128,4096]{1,0:T(8,128)(2,1)S(1)}, u32[]{:S(2)}, u32[]{:S(2)}) %collective-permute-start.19) | collective-permute-done | bytes 1048608 | tf_op jit(solution)/shard_map/ppermute | solution.py:46
  440.6 6.5 %collective-permute-done.23 = bf16[128,4096]{1,0:T(8,128)(2,1)S(1)} collective-permute-done((bf16[128,4096]{1,0:T(8,128)(2,1)S(1)}, bf16[128,4096]{1,0:T(8,128)(2,1)S(1)}, u32[]{:S(2)}, u32[]{:S(2)}) %collective-permute-start.23) | collective-permute-done | bytes 1048608 | tf_op jit(solution)/shard_map/ppermute | solution.py:46
  502.3 47.1 %collective-permute-done.2 = bf16[128,1024]{1,0:T(8,128)(2,1)S(1)} collective-permute-done((bf16[128,1024]{1,0:T(8,128)(2,1)S(1)}, bf16[128,1024]{1,0:T(8,128)(2,1)S(1)}, u32[]{:S(2)}, u32[]{:S(2)}) %collective-permute-start.2) | collective-permute-done | bytes 262176 | tf_op jit(solution)/shard_map/ppermute | solution.py:46
  550.0 6.1 %collective-permute-done.6 = bf16[128,1024]{1,0:T(8,128)(2,1)S(1)} collective-permute-done((bf16[128,1024]{1,0:T(8,128)(2,1)S(1)}, bf16[128,1024]{1,0:T(8,128)(2,1)S(1)}, u32[]{:S(2)}, u32[]{:S(2)}) %collective-permute-start.6) | collective-permute-done | bytes 262176 | tf_op jit(solution)/shard_map/ppermute | solution.py:46
  (260 shorter events, 216.9 us)
Async XLA Ops:
  6.7 55.5 %all-to-all-start = ((bf16[8,1024,128]{1,2,0:T(8,128)(2,1)}), bf16[8,1024,128]{1,2,0:T(8,128)(2,1)}, u32[]{:S(2)}, u32[]{:S(2)}) async-start(bf16[8,1024,128]{1,2,0:T(8,128)(2,1)} %bitcast.99), calls=%async_computation | async-start | bytes 4194304 | tf_op jit(solution)/shard_map/all_to_all | solution.py:40
  62.2 53.6 %all-to-all-start.2 = ((bf16[8,1024,128]{2,1,0:T(8,128)(2,1)}), bf16[8,1024,128]{2,1,0:T(8,128)(2,1)}, u32[]{:S(2)}, u32[]{:S(2)}) async-start(bf16[8,1024,128]{2,1,0:T(8,128)(2,1)} %bitcast.98), calls=%async_computation.2 | async-start | bytes 4194304 | tf_op jit(solution)/shard_map/all_to_all | solution.py:40
  119.1 111.0 %all-to-all-start.1 = ((bf16[8,1024,128]{2,1,0:T(8,128)(2,1)}), bf16[8,1024,128]{2,1,0:T(8,128)(2,1)}, u32[]{:S(2)}, u32[]{:S(2)}) async-start(bf16[8,1024,128]{2,1,0:T(8,128)(2,1)} %bitcast_bitcast_fusion), calls=%async_computation.1 | async-start | bytes 4194304 | tf_op jit(solution)/shard_map/all_to_all | solution.py:40
  155.1 45.2 %collective-permute-start.32 = (bf16[512,1024]{1,0:T(8,128)(2,1)S(1)}, bf16[512,1024]{1,0:T(8,128)(2,1)S(1)}, u32[]{:S(2)}, u32[]{:S(2)}) collective-permute-start(bf16[512,1024]{1,0:T(8,128)(2,1)S(1)} %convolution_convert_fusion.11), channel_id=1, source_target_pairs={{0,8},{8,0},{16,24},{24,16},{1,9},{9,1},{17,25},{25,17},{2,10},{10... | collective-permute-start | bytes 3145736 | tf_op jit(solution)/shard_map/ppermute | solution.py:46
  157.0 46.3 %collective-permute-start.28 = (bf16[512,1024]{1,0:T(8,128)(2,1)S(1)}, bf16[512,1024]{1,0:T(8,128)(2,1)S(1)}, u32[]{:S(2)}, u32[]{:S(2)}) collective-permute-start(bf16[512,1024]{1,0:T(8,128)(2,1)S(1)} %convolution_convert_fusion.12), channel_id=1, source_target_pairs={{0,16},{8,24},{16,0},{24,8},{1,17},{9,25},{17,1},{25,9},{2,18},{10... | collective-permute-start | bytes 3145736 | tf_op jit(solution)/shard_map/ppermute | solution.py:46
  162.9 43.3 %collective-permute-start.36 = (bf16[512,1024]{1,0:T(8,128)(2,1)S(1)}, bf16[512,1024]{1,0:T(8,128)(2,1)S(1)}, u32[]{:S(2)}, u32[]{:S(2)}) collective-permute-start(bf16[512,1024]{1,0:T(8,128)(2,1)S(1)} %convolution_convert_fusion.10), channel_id=1, source_target_pairs={{0,16},{8,24},{16,0},{24,8},{1,17},{9,25},{17,1},{25,9},{2,18},{10... | collective-permute-start | bytes 3145736 | tf_op jit(solution)/shard_map/ppermute | solution.py:46
  179.7 37.2 %collective-permute-start.25 = (bf16[256,1024]{1,0:T(8,128)(2,1)S(1)}, bf16[256,1024]{1,0:T(8,128)(2,1)S(1)}, u32[]{:S(2)}, u32[]{:S(2)}) collective-permute-start(bf16[256,1024]{1,0:T(8,128)(2,1)S(1)} %dynamic-slice_convert_fusion.3), channel_id=1, source_target_pairs={{0,16},{8,24},{16,0},{24,8},{1,17},{9,25},{17,1},{25,9},{2,18},{10... | collective-permute-start | bytes 1572872 | tf_op jit(solution)/shard_map/ppermute | solution.py:46
  239.4 43.3 %collective-permute-start.44 = (bf16[256,1024]{1,0:T(8,128)(2,1)}, bf16[256,1024]{1,0:T(8,128)(2,1)}, u32[]{:S(2)}, u32[]{:S(2)}) collective-permute-start(bf16[256,1024]{1,0:T(8,128)(2,1)} %convolution_convert_fusion.14), channel_id=1, source_target_pairs={{0,16},{8,24},{16,0},{24,8},{1,17},{9,25},{17,1},{25,9},{2,18},{10... | collective-permute-start | bytes 1572872 | tf_op jit(solution)/shard_map/ppermute | solution.py:46
  240.6 44.5 %collective-permute-start.40 = (bf16[256,1024]{1,0:T(8,128)(2,1)}, bf16[256,1024]{1,0:T(8,128)(2,1)}, u32[]{:S(2)}, u32[]{:S(2)}) collective-permute-start(bf16[256,1024]{1,0:T(8,128)(2,1)} %convolution_convert_fusion.15), channel_id=1, source_target_pairs={{0,8},{8,0},{16,24},{24,16},{1,9},{9,1},{17,25},{25,17},{2,10},{10... | collective-permute-start | bytes 1572872 | tf_op jit(solution)/shard_map/ppermute | solution.py:46
  261.5 53.3 %collective-permute-start.8 = (bf16[128,4096]{1,0:T(8,128)(2,1)}, bf16[128,4096]{1,0:T(8,128)(2,1)}, u32[]{:S(2)}, u32[]{:S(2)}) collective-permute-start(bf16[128,4096]{1,0:T(8,128)(2,1)} %convolution_convert_fusion.3), channel_id=1, source_target_pairs={{0,8},{8,0},{16,24},{24,16},{1,9},{9,1},{17,25},{25,17},{2,10},{10... | collective-permute-start | bytes 3145736 | tf_op jit(solution)/shard_map/ppermute | solution.py:46
  262.0 59.0 %collective-permute-start.16 = (bf16[128,4096]{1,0:T(8,128)(2,1)}, bf16[128,4096]{1,0:T(8,128)(2,1)}, u32[]{:S(2)}, u32[]{:S(2)}) collective-permute-start(bf16[128,4096]{1,0:T(8,128)(2,1)} %convolution_convert_fusion.1), channel_id=1, source_target_pairs={{0,8},{8,0},{16,24},{24,16},{1,9},{9,1},{17,25},{25,17},{2,10},{10... | collective-permute-start | bytes 3145736 | tf_op jit(solution)/shard_map/ppermute | solution.py:46
  267.4 182.1 %all-to-all-start.3 = ((bf16[8,1024,128]{2,1,0:T(8,128)(2,1)}), bf16[8,1024,128]{2,1,0:T(8,128)(2,1)}, u32[]{:S(2)}, u32[]{:S(2)}) async-start(bf16[8,1024,128]{2,1,0:T(8,128)(2,1)} %bitcast.97), calls=%async_computation.3 | async-start | bytes 4194304 | tf_op jit(solution)/shard_map/all_to_all | solution.py:40
  318.9 39.1 %collective-permute-start.9 = (bf16[64,4096]{1,0:T(8,128)(2,1)S(1)}, bf16[64,4096]{1,0:T(8,128)(2,1)S(1)}, u32[]{:S(2)}, u32[]{:S(2)}) collective-permute-start(bf16[64,4096]{1,0:T(8,128)(2,1)S(1)} %dynamic-slice_convert_fusion.7), channel_id=1, source_target_pairs={{0,16},{8,24},{16,0},{24,8},{1,17},{9,25},{17,1},{25,9},{2,18},{10... | collective-permute-start | bytes 1572872 | tf_op jit(solution)/shard_map/ppermute | solution.py:46
  321.1 38.5 %collective-permute-start.13 = (bf16[64,4096]{1,0:T(8,128)(2,1)S(1)}, bf16[64,4096]{1,0:T(8,128)(2,1)S(1)}, u32[]{:S(2)}, u32[]{:S(2)}) collective-permute-start(bf16[64,4096]{1,0:T(8,128)(2,1)S(1)} %dynamic-slice_convert_fusion.6), channel_id=1, source_target_pairs={{0,8},{8,0},{16,24},{24,16},{1,9},{9,1},{17,25},{25,17},{2,10},{10... | collective-permute-start | bytes 1572872 | tf_op jit(solution)/shard_map/ppermute | solution.py:46
  346.7 33.7 %collective-permute-start.47 = (bf16[256,1024]{1,0:T(8,128)(2,1)S(1)}, bf16[256,1024]{1,0:T(8,128)(2,1)S(1)}, u32[]{:S(2)}, u32[]{:S(2)}) collective-permute-start(bf16[256,1024]{1,0:T(8,128)(2,1)S(1)} %pad_maximum_fusion.13), channel_id=1, source_target_pairs={{0,16},{8,24},{16,0},{24,8},{1,17},{9,25},{17,1},{25,9},{2,18},{10... | collective-permute-start | bytes 1572872 | tf_op jit(solution)/shard_map/ppermute | solution.py:46
  359.5 32.1 %collective-permute-start.10 = (bf16[64,4096]{1,0:T(8,128)(2,1)S(1)}, bf16[64,4096]{1,0:T(8,128)(2,1)S(1)}, u32[]{:S(2)}, u32[]{:S(2)}) collective-permute-start(bf16[64,4096]{1,0:T(8,128)(2,1)S(1)} %add_convert_fusion.7), channel_id=1, source_target_pairs={{0,16},{8,24},{16,0},{24,8},{1,17},{9,25},{17,1},{25,9},{2,18},{10... | collective-permute-start | bytes 1572872 | tf_op jit(solution)/shard_map/ppermute | solution.py:46
  370.8 32.1 %collective-permute-start.18 = (bf16[64,4096]{1,0:T(8,128)(2,1)S(1)}, bf16[64,4096]{1,0:T(8,128)(2,1)S(1)}, u32[]{:S(2)}, u32[]{:S(2)}) collective-permute-start(bf16[64,4096]{1,0:T(8,128)(2,1)S(1)} %add_convert_fusion.5), channel_id=1, source_target_pairs={{0,16},{8,24},{16,0},{24,8},{1,17},{9,25},{17,1},{25,9},{2,18},{10... | collective-permute-start | bytes 1572872 | tf_op jit(solution)/shard_map/ppermute | solution.py:46
  403.0 35.1 %collective-permute-start.19 = (bf16[128,4096]{1,0:T(8,128)(2,1)S(1)}, bf16[128,4096]{1,0:T(8,128)(2,1)S(1)}, u32[]{:S(2)}, u32[]{:S(2)}) collective-permute-start(bf16[128,4096]{1,0:T(8,128)(2,1)S(1)} %pad_maximum_fusion.4), channel_id=1, source_target_pairs={{0,8},{8,0},{16,24},{24,16},{1,9},{9,1},{17,25},{25,17},{2,10},{10... | collective-permute-start | bytes 3145736 | tf_op jit(solution)/shard_map/ppermute | solution.py:46
  404.8 42.3 %collective-permute-start.23 = (bf16[128,4096]{1,0:T(8,128)(2,1)S(1)}, bf16[128,4096]{1,0:T(8,128)(2,1)S(1)}, u32[]{:S(2)}, u32[]{:S(2)}) collective-permute-start(bf16[128,4096]{1,0:T(8,128)(2,1)S(1)} %pad_maximum_fusion.5), channel_id=1, source_target_pairs={{0,16},{8,24},{16,0},{24,8},{1,17},{9,25},{17,1},{25,9},{2,18},{10... | collective-permute-start | bytes 3145736 | tf_op jit(solution)/shard_map/ppermute | solution.py:46
  484.0 76.1 %collective-permute-start.39 = (bf16[512,1024]{1,0:T(8,128)(2,1)S(1)}, bf16[512,1024]{1,0:T(8,128)(2,1)S(1)}, u32[]{:S(2)}, u32[]{:S(2)}) collective-permute-start(bf16[512,1024]{1,0:T(8,128)(2,1)S(1)} %pad_maximum_fusion.9), channel_id=1, source_target_pairs={{0,16},{8,24},{16,0},{24,8},{1,17},{9,25},{17,1},{25,9},{2,18},{10... | collective-permute-start | bytes 3145736 | tf_op jit(solution)/shard_map/ppermute | solution.py:46
  490.6 66.1 %collective-permute-start.27 = (bf16[512,1024]{1,0:T(8,128)(2,1)S(1)}, bf16[512,1024]{1,0:T(8,128)(2,1)S(1)}, u32[]{:S(2)}, u32[]{:S(2)}) collective-permute-start(bf16[512,1024]{1,0:T(8,128)(2,1)S(1)} %pad_maximum_fusion.6), channel_id=1, source_target_pairs={{0,8},{8,0},{16,24},{24,16},{1,9},{9,1},{17,25},{25,17},{2,10},{10... | collective-permute-start | bytes 3145736 | tf_op jit(solution)/shard_map/ppermute | solution.py:46
  495.1 63.3 %collective-permute-start.31 = (bf16[512,1024]{1,0:T(8,128)(2,1)S(1)}, bf16[512,1024]{1,0:T(8,128)(2,1)S(1)}, u32[]{:S(2)}, u32[]{:S(2)}) collective-permute-start(bf16[512,1024]{1,0:T(8,128)(2,1)S(1)} %pad_maximum_fusion.7), channel_id=1, source_target_pairs={{0,16},{8,24},{16,0},{24,8},{1,17},{9,25},{17,1},{25,9},{2,18},{10... | collective-permute-start | bytes 3145736 | tf_op jit(solution)/shard_map/ppermute | solution.py:46
  500.8 48.6 %collective-permute-start.2 = (bf16[128,1024]{1,0:T(8,128)(2,1)S(1)}, bf16[128,1024]{1,0:T(8,128)(2,1)S(1)}, u32[]{:S(2)}, u32[]{:S(2)}) collective-permute-start(bf16[128,1024]{1,0:T(8,128)(2,1)S(1)} %add_convert_fusion.11), channel_id=1, source_target_pairs={{0,16},{8,24},{16,0},{24,8},{1,17},{9,25},{17,1},{25,9},{2,18},{10... | collective-permute-start | bytes 786440 | tf_op jit(solution)/shard_map/ppermute | solution.py:46
  501.5 57.8 %collective-permute-start.35 = (bf16[512,1024]{1,0:T(8,128)(2,1)S(1)}, bf16[512,1024]{1,0:T(8,128)(2,1)S(1)}, u32[]{:S(2)}, u32[]{:S(2)}) collective-permute-start(bf16[512,1024]{1,0:T(8,128)(2,1)S(1)} %pad_maximum_fusion.8), channel_id=1, source_target_pairs={{0,8},{8,0},{16,24},{24,16},{1,9},{9,1},{17,25},{25,17},{2,10},{10... | collective-permute-start | bytes 3145736 | tf_op jit(solution)/shard_map/ppermute | solution.py:46
  (58 other events, 884.3 us)

commit v3 on v2

--- a/solution.py
+++ b/solution.py
@@ -46,14 +46,10 @@
     return lax.ppermute(values, "dp", [(i, i ^ (1 << bit)) for i in range(size)])
 
 
-def start_sum(left, right, bits):
-    me = lax.axis_index("dp")
+def half_of(left, bit, away):
     half = left.shape[1] // 2
-    mine = (me >> bits[0]) & 1
-    away = dot(lax.dynamic_slice_in_dim(left, (1 - mine) * half, half, 1), right, 0, 0).astype(BF16)
-    got = exchange(away, bits[0])
-    kept = dot(lax.dynamic_slice_in_dim(left, mine * half, half, 1), right, 0, 0)
-    return kept + got.astype(F32)
+    mine = (lax.axis_index("dp") >> bit) & 1
+    return lax.dynamic_slice_in_dim(left, (1 - mine if away else mine) * half, half, 1)
 
 
 def scatter_sum(total, bits):
@@ -83,15 +79,26 @@
     return [bits if piece % 2 == 0 else bits[::-1] for piece in range(pieces)]
 
 
-def reduced_product(left, right, pieces):
+def cuts(left, pieces):
     rows = left.shape[1] // pieces
+    return [lax.slice_in_dim(left, p * rows, (p + 1) * rows, axis=1) for p in range(pieces)]
+
+
+def send_products(left, right, pieces):
+    orders = piece_orders(pieces)
+    away = [
+        dot(half_of(cut, order[0], True), right, 0, 0).astype(BF16)
+        for cut, order in zip(cuts(left, pieces), orders)
+    ]
+    return away, [exchange(part, order[0]) for part, order in zip(away, orders)]
+
+
+def own_shares(left, right, came):
+    orders = piece_orders(len(came))
     out = []
-    for piece, order in enumerate(piece_orders(pieces)):
-        cut = lax.slice_in_dim(left, piece * rows, (piece + 1) * rows, axis=1)
-        if order:
-            out.append(scatter_sum(start_sum(cut, right, order), order))
-        else:
-            out.append(dot(cut, right, 0, 0).astype(BF16))
+    for cut, order, got in zip(cuts(left, len(came)), orders, came):
+        kept = dot(half_of(cut, order[0], False), right, 0, 0)
+        out.append(scatter_sum(kept + got.astype(F32), order))
     return out
 
 
@@ -113,15 +120,22 @@
     back_third = after(back_third, third)
     mixed_down = swap_blocks(third, blocks)
 
-    share_left_down = reduced_product(hidden, back_third, 4)
+    away_left_down, came_left_down = send_products(hidden, back_third, 4)
+    back_third = after(back_third, *away_left_down)
     back_hidden = dot(back_third, left_down, 1, 1)
     back_pre = jax.vjp(gelu_tanh, pre_act)[1](back_hidden)[0].astype(BF16)
     back_pre = after(back_pre, mixed_down)
+    came_left_down = [after(got, back_pre) for got in came_left_down]
+    share_left_down = own_shares(hidden, back_third, came_left_down)
     back_mixed_up = dot(back_pre, right_up, 1, 1).astype(BF16)
     back_first = swap_blocks(back_mixed_up, blocks)
-    share_right_up = reduced_product(mixed_up, back_pre, 4)
-    share_right_down = reduced_product(mixed_down, out_grad, 2)
-    share_left_up = reduced_product(tokens_in, back_first, 2)
+    _, came_right_up = send_products(mixed_up, back_pre, 4)
+    came_right_up = [after(got, back_first) for got in came_right_up]
+    share_right_up = own_shares(mixed_up, back_pre, came_right_up)
+    _, came_right_down = send_products(mixed_down, out_grad, 2)
+    share_right_down = own_shares(mixed_down, out_grad, came_right_down)
+    _, came_left_up = send_products(tokens_in, back_first, 2)
+    share_left_up = own_shares(tokens_in, back_first, came_left_up)
     share_left_down = [after(share, back_first) for share in share_left_down]
 
     layer_out = dot(mixed_down, right_down, 1, 0).astype(BF16)

time: 575 us -> 589 us (1.024)
  waiting for transfers between devices: 295 us -> 256 us
  matrix products: 145 us -> 171 us
  other arithmetic: 26.5 us -> 38.6 us
  local copies, waits for them, and re-layouts: 31.3 us -> 41.3 us
    ppermute x48, waiting for transfers between devices: 246 us -> 196 us  [exchange(): return lax.ppermute(values, 'dp', [(i, i ^ 1 << bit) for i in range(size)])]
    dot_general x32, matrix products: 145 us -> 171 us  [dot(): lax.dot_general(left, right, (((left_dim,), (right_dim,)), ((), ())), pre...]
    add x0 -> x8, other arithmetic: none -> 20.2 us  [own_shares(): out.append(scatter_sum(kept + got.astype(F32), order))]
    all_to_all x4, waiting for transfers between devices: 49.3 us -> 59.3 us  [swap_blocks(): lax.all_to_all(parts, 'tensor', split_axis=0, concat_axis=0, tiled=True)]
    unnamed x16, other arithmetic: 11.4 us -> 4.6 us
  transfers between devices with their start and end apart: 52 -> 52, of which waited for: 27 -> 27; matrix products, arithmetic and copies ran while one was open for 31% -> 37% of each run, Pallas kernels for 0% -> 0%
where the time goes in v3:
time: 589 us; the launch traced here: 584 us
  waiting for transfers between devices  256 us (43%)
  matrix products  171 us (29%)
  starting transfers between devices  75.1 us (13%)
  local copies, waits for them, and re-layouts  41.3 us (7%)
  other arithmetic  38.6 us (7%)
    ppermute x48, waiting for transfers between devices, exchange(): return lax.ppermute(values, 'dp', [(i, i ^ 1 << bit) for i in range(size)])  196 us
    dot_general x32, matrix products, dot(): lax.dot_general(left, right, (((left_dim,), (right_dim,)), ((), ())), pre...  171 us
    all_to_all x4, waiting for transfers between devices, swap_blocks(): lax.all_to_all(parts, 'tensor', split_axis=0, concat_axis=0, tiled=True)  59.3 us
    ppermute x48, starting transfers between devices, exchange(): return lax.ppermute(values, 'dp', [(i, i ^ 1 << bit) for i in range(size)])  54.7 us
    all_to_all x4, starting transfers between devices, swap_blocks(): lax.all_to_all(parts, 'tensor', split_axis=0, concat_axis=0, tiled=True)  20.4 us
    add x8, other arithmetic, own_shares(): out.append(scatter_sum(kept + got.astype(F32), order))  20.2 us
  transfers between devices with their start and end apart: 52, of which 27 were waited for; matrix products, arithmetic and copies ran while one was open for 37% of the time, Pallas kernels for 0%

profile of v3, /device:TPU:0, one launch (start us, length us, event | category | flops | bytes accessed | tf_op | source)
XLA Modules:
  0.0 583.6 jit_solution(13306408164748166007)
XLA Ops:
  0.6 6.1 %convolution_convert_fusion.9 = bf16[1024,1024]{0,1:T(8,128)(2,1)} fusion(bf16[1024,1024]{1,0:T(8,128)(2,1)} %param.6, bf16[1024,1024]{1,0:T(8,128)(2,1)} %param.8), kind=kOutput, calls=%fused_computation.33 | convolution fusion | flops 2148532224 | bytes 6291456 | tf_op jit(solution)/shard_map/dot_general | solution.py:16
  6.7 6.3 %all-to-all-start = ((bf16[8,1024,128]{1,2,0:T(8,128)(2,1)}), bf16[8,1024,128]{1,2,0:T(8,128)(2,1)}, u32[]{:S(2)}, u32[]{:S(2)}) async-start(bf16[8,1024,128]{1,2,0:T(8,128)(2,1)} %bitcast.99), calls=%async_computation | async-start | bytes 4194304 | tf_op jit(solution)/shard_map/all_to_all | solution.py:40
  25.2 37.0 %all-to-all-done = bf16[8,1024,128]{1,2,0:T(8,128)(2,1)} async-done(((bf16[8,1024,128]{1,2,0:T(8,128)(2,1)}), bf16[8,1024,128]{1,2,0:T(8,128)(2,1)}, u32[]{:S(2)}, u32[]{:S(2)}) %all-to-all-start) | async-done | bytes 2097184 | tf_op jit(solution)/shard_map/all_to_all | solution.py:40
  66.8 20.2 %multiply_convert_fusion = (bf16[1024,4096]{1,0:T(8,128)(2,1)S(1)}, f32[1024,4096]{1,0:T(8,128)}) fusion(bf16[1024,1024]{0,1:T(8,128)(2,1)} %bitcast.3, bf16[1024,4096]{1,0:T(8,128)(2,1)} %param.9), kind=kOutput, calls=%fused_computation.9 | convolution fusion | flops 8627683328 | bytes 35651584 | tf_op jit(solution)/shard_map/dot_general | solution.py:16
  86.9 11.2 %convolution_convert_fusion.5.refs_1_ = bf16[1024,1024]{1,0:T(8,128)(2,1)S(1)} fusion(bf16[1024,4096]{1,0:T(8,128)(2,1)S(1)} %get-tuple-element.50, bf16[4096,1024]{1,0:T(8,128)(2,1)} %param.10), kind=kOutput, calls=%fused_computation.29 | convolution fusion | flops 8590983168 | bytes 18874368 | tf_op jit(solution)/shard_map/dot_general | solution.py:16
  103.7 12.1 %all-to-all-done.2 = bf16[8,1024,128]{2,1,0:T(8,128)(2,1)} async-done(((bf16[8,1024,128]{2,1,0:T(8,128)(2,1)}), bf16[8,1024,128]{2,1,0:T(8,128)(2,1)}, u32[]{:S(2)}, u32[]{:S(2)}) %all-to-all-start.2) | async-done | bytes 2097184 | tf_op jit(solution)/shard_map/all_to_all | solution.py:40
  156.5 24.7 %fusion.6.refs_0_ = bf16[1024,4096]{1,0:T(8,128)(2,1)} fusion(f32[1024,4096]{1,0:T(8,128)} %get-tuple-element.51, bf16[1024,1024]{1,0:T(8,128)(2,1)} %shard_map.110, bf16[4096,1024]{1,0:T(8,128)(2,1)} %param.10), kind=kOutput, calls=%fused_computation.8 | convolution fusion | flops 8673820672 | bytes 35651584 | tf_op jit(solution)/shard_map/dot_general | solution.py:16
  181.2 10.2 %all-to-all-done.1 = bf16[8,1024,128]{2,1,0:T(8,128)(2,1)} async-done(((bf16[8,1024,128]{2,1,0:T(8,128)(2,1)}), bf16[8,1024,128]{2,1,0:T(8,128)(2,1)}, u32[]{:S(2)}, u32[]{:S(2)}) %all-to-all-start.1) | async-done | bytes 2097184 | tf_op jit(solution)/shard_map/all_to_all | solution.py:40
  194.6 15.0 %convolution_convert_fusion.4 = bf16[1024,1024]{0,1:T(8,128)(2,1)} fusion(bf16[1024,4096]{1,0:T(8,128)(2,1)} %shard_map.111.refs_1_, bf16[1024,4096]{1,0:T(8,128)(2,1)} %param.9), kind=kOutput, calls=%fused_computation.28 | convolution fusion | flops 8590983168 | bytes 18874368 | tf_op jit(solution)/shard_map/dot_general | solution.py:16
  254.4 6.1 %fusion.46 = f32[128,4096]{1,0:T(8,128)} fusion(bf16[1024,4096]{1,0:T(8,128)(2,1)} %shard_map.111.refs_1_, bf16[1024,256]{0,1:T(8,128)(2,1)} %get-tuple-element.14, s32[]{:T(128)S(6)} %select_n.308), kind=kOutput, calls=%fused_computation.153 | convolution fusion | flops 1073741824 | bytes 10747908 | tf_op jit(solution)/shard_map/dot_general | solution.py:16
  260.5 6.0 %fusion.40 = f32[128,4096]{1,0:T(8,128)} fusion(bf16[1024,4096]{1,0:T(8,128)(2,1)} %shard_map.111.refs_1_, bf16[1024,256]{0,1:T(8,128)(2,1)S(1)} %copy-done.35, s32[]{:T(128)S(6)} %select_n.308), kind=kOutput, calls=%fused_computation.147 | convolution fusion | flops 1073741824 | bytes 10747908 | tf_op jit(solution)/shard_map/dot_general | solution.py:16
  268.7 6.0 %convolution_convert_fusion.8 = bf16[1024,1024]{1,0:T(8,128)(2,1)} fusion(bf16[1024,1024]{1,0:T(8,128)(2,1)S(1)} %copy-done, bf16[8,1024,128]{2,1,0:T(8,128)(2,1)} %all-to-all-done.1), kind=kOutput, calls=%fused_computation.32 | convolution fusion | flops 2148532224 | bytes 6291456 | tf_op jit(solution)/shard_map/dot_general | solution.py:16
  284.0 17.5 %collective-permute-done.40 = bf16[256,1024]{1,0:T(8,128)(2,1)} collective-permute-done((bf16[256,1024]{1,0:T(8,128)(2,1)}, bf16[256,1024]{1,0:T(8,128)(2,1)}, u32[]{:S(2)}, u32[]{:S(2)}) %collective-permute-start.40) | collective-permute-done | bytes 524320 | tf_op jit(solution)/shard_map/ppermute | solution.py:46
  320.3 16.7 %collective-permute-done.46 = bf16[128,1024]{1,0:T(8,128)(2,1)S(1)} collective-permute-done((bf16[128,1024]{1,0:T(8,128)(2,1)S(1)}, bf16[128,1024]{1,0:T(8,128)(2,1)S(1)}, u32[]{:S(2)}, u32[]{:S(2)}) %collective-permute-start.46) | collective-permute-done | bytes 262176 | tf_op jit(solution)/shard_map/ppermute | solution.py:46
  338.6 6.6 %collective-permute-done.42 = bf16[128,1024]{1,0:T(8,128)(2,1)S(1)} collective-permute-done((bf16[128,1024]{1,0:T(8,128)(2,1)S(1)}, bf16[128,1024]{1,0:T(8,128)(2,1)S(1)}, u32[]{:S(2)}, u32[]{:S(2)}) %collective-permute-start.42) | collective-permute-done | bytes 262176 | tf_op jit(solution)/shard_map/ppermute | solution.py:46
  373.8 10.6 %collective-permute-done.16.refs_0_ = bf16[128,4096]{1,0:T(8,128)(2,1)} collective-permute-done((bf16[128,4096]{1,0:T(8,128)(2,1)}, bf16[128,4096]{1,0:T(8,128)(2,1)}, u32[]{:S(2)}, u32[]{:S(2)}) %collective-permute-start.16) | collective-permute-done | bytes 1048608 | tf_op jit(solution)/shard_map/ppermute | solution.py:46
  415.6 6.4 %collective-permute-done.21 = bf16[64,4096]{1,0:T(8,128)(2,1)S(1)} collective-permute-done((bf16[64,4096]{1,0:T(8,128)(2,1)S(1)}, bf16[64,4096]{1,0:T(8,128)(2,1)S(1)}, u32[]{:S(2)}, u32[]{:S(2)}) %collective-permute-start.21) | collective-permute-done | bytes 524320 | tf_op jit(solution)/shard_map/ppermute | solution.py:46
  436.7 14.6 %collective-permute-done.34 = bf16[256,1024]{1,0:T(8,128)(2,1)S(1)} collective-permute-done((bf16[256,1024]{1,0:T(8,128)(2,1)S(1)}, bf16[256,1024]{1,0:T(8,128)(2,1)S(1)}, u32[]{:S(2)}, u32[]{:S(2)}) %collective-permute-start.34) | collective-permute-done | bytes 524320 | tf_op jit(solution)/shard_map/ppermute | solution.py:46
  461.0 10.8 %collective-permute-done.14 = bf16[64,4096]{1,0:T(8,128)(2,1)S(1)} collective-permute-done((bf16[64,4096]{1,0:T(8,128)(2,1)S(1)}, bf16[64,4096]{1,0:T(8,128)(2,1)S(1)}, u32[]{:S(2)}, u32[]{:S(2)}) %collective-permute-start.14) | collective-permute-done | bytes 524320 | tf_op jit(solution)/shard_map/ppermute | solution.py:46
  484.8 23.5 %collective-permute-done.6 = bf16[128,1024]{1,0:T(8,128)(2,1)S(1)} collective-permute-done((bf16[128,1024]{1,0:T(8,128)(2,1)S(1)}, bf16[128,1024]{1,0:T(8,128)(2,1)S(1)}, u32[]{:S(2)}, u32[]{:S(2)}) %collective-permute-start.6) | collective-permute-done | bytes 262176 | tf_op jit(solution)/shard_map/ppermute | solution.py:46
  516.6 17.9 %collective-permute-done.35 = bf16[512,1024]{1,0:T(8,128)(2,1)S(1)} collective-permute-done((bf16[512,1024]{1,0:T(8,128)(2,1)S(1)}, bf16[512,1024]{1,0:T(8,128)(2,1)S(1)}, u32[]{:S(2)}, u32[]{:S(2)}) %collective-permute-start.35) | collective-permute-done | bytes 1048608 | tf_op jit(solution)/shard_map/ppermute | solution.py:46
  538.0 7.6 %collective-permute-done.3 = bf16[256,1024]{1,0:T(8,128)(2,1)S(1)} collective-permute-done((bf16[256,1024]{1,0:T(8,128)(2,1)S(1)}, bf16[256,1024]{1,0:T(8,128)(2,1)S(1)}, u32[]{:S(2)}, u32[]{:S(2)}) %collective-permute-start.3) | collective-permute-done | bytes 524320 | tf_op jit(solution)/shard_map/ppermute | solution.py:46
  548.0 17.6 %collective-permute-done.11 = bf16[128,4096]{1,0:T(8,128)(2,1)S(1)} collective-permute-done((bf16[128,4096]{1,0:T(8,128)(2,1)S(1)}, bf16[128,4096]{1,0:T(8,128)(2,1)S(1)}, u32[]{:S(2)}, u32[]{:S(2)}) %collective-permute-start.11) | collective-permute-done | bytes 1048608 | tf_op jit(solution)/shard_map/ppermute | solution.py:46
  568.8 8.1 %collective-permute-done.19 = bf16[128,4096]{1,0:T(8,128)(2,1)S(1)} collective-permute-done((bf16[128,4096]{1,0:T(8,128)(2,1)S(1)}, bf16[128,4096]{1,0:T(8,128)(2,1)S(1)}, u32[]{:S(2)}, u32[]{:S(2)}) %collective-permute-start.19) | collective-permute-done | bytes 1048608 | tf_op jit(solution)/shard_map/ppermute | solution.py:46
  (315 shorter events, 263.1 us)
Async XLA Ops:
  6.7 55.5 %all-to-all-start = ((bf16[8,1024,128]{1,2,0:T(8,128)(2,1)}), bf16[8,1024,128]{1,2,0:T(8,128)(2,1)}, u32[]{:S(2)}, u32[]{:S(2)}) async-start(bf16[8,1024,128]{1,2,0:T(8,128)(2,1)} %bitcast.99), calls=%async_computation | async-start | bytes 4194304 | tf_op jit(solution)/shard_map/all_to_all | solution.py:40
  62.2 53.6 %all-to-all-start.2 = ((bf16[8,1024,128]{2,1,0:T(8,128)(2,1)}), bf16[8,1024,128]{2,1,0:T(8,128)(2,1)}, u32[]{:S(2)}, u32[]{:S(2)}) async-start(bf16[8,1024,128]{2,1,0:T(8,128)(2,1)} %bitcast.98), calls=%async_computation.2 | async-start | bytes 4194304 | tf_op jit(solution)/shard_map/all_to_all | solution.py:40
  137.6 53.8 %all-to-all-start.1 = ((bf16[8,1024,128]{2,1,0:T(8,128)(2,1)}), bf16[8,1024,128]{2,1,0:T(8,128)(2,1)}, u32[]{:S(2)}, u32[]{:S(2)}) async-start(bf16[8,1024,128]{2,1,0:T(8,128)(2,1)} %bitcast_bitcast_fusion), calls=%async_computation.1 | async-start | bytes 4194304 | tf_op jit(solution)/shard_map/all_to_all | solution.py:40
  149.6 127.0 %collective-permute-start.24 = (bf16[512,1024]{1,0:T(8,128)(2,1)}, bf16[512,1024]{1,0:T(8,128)(2,1)S(1)}, u32[]{:S(2)}, u32[]{:S(2)}) collective-permute-start(bf16[512,1024]{1,0:T(8,128)(2,1)} %convolution_convert_fusion.13.refs_1_), channel_id=1, source_target_pairs={{0,8},{8,0},{16,24},{24,16},{1,9},{9,1},{17,25},{25,17},{2,10},{10... | collective-permute-start | bytes 3145736 | tf_op jit(solution)/shard_map/ppermute | solution.py:46
  151.1 115.4 %collective-permute-start.32 = (bf16[512,1024]{1,0:T(8,128)(2,1)}, bf16[512,1024]{1,0:T(8,128)(2,1)}, u32[]{:S(2)}, u32[]{:S(2)}) collective-permute-start(bf16[512,1024]{1,0:T(8,128)(2,1)} %convolution_convert_fusion.11.refs_3_), channel_id=1, source_target_pairs={{0,8},{8,0},{16,24},{24,16},{1,9},{9,1},{17,25},{25,17},{2,10},{10... | collective-permute-start | bytes 3145736 | tf_op jit(solution)/shard_map/ppermute | solution.py:46
  151.6 59.5 %collective-permute-start.28 = (bf16[512,1024]{1,0:T(8,128)(2,1)}, bf16[512,1024]{1,0:T(8,128)(2,1)}, u32[]{:S(2)}, u32[]{:S(2)}) collective-permute-start(bf16[512,1024]{1,0:T(8,128)(2,1)} %convolution_convert_fusion.12.refs_2_), channel_id=1, source_target_pairs={{0,16},{8,24},{16,0},{24,8},{1,17},{9,25},{17,1},{25,9},{2,18},{10... | collective-permute-start | bytes 3145736 | tf_op jit(solution)/shard_map/ppermute | solution.py:46
  153.2 76.6 %collective-permute-start.36 = (bf16[512,1024]{1,0:T(8,128)(2,1)}, bf16[512,1024]{1,0:T(8,128)(2,1)}, u32[]{:S(2)}, u32[]{:S(2)}) collective-permute-start(bf16[512,1024]{1,0:T(8,128)(2,1)} %convolution_convert_fusion.10.refs_4_), channel_id=1, source_target_pairs={{0,16},{8,24},{16,0},{24,8},{1,17},{9,25},{17,1},{25,9},{2,18},{10... | collective-permute-start | bytes 3145736 | tf_op jit(solution)/shard_map/ppermute | solution.py:46
  233.0 70.9 %collective-permute-start.37 = (bf16[256,1024]{1,0:T(8,128)(2,1)}, bf16[256,1024]{1,0:T(8,128)(2,1)}, u32[]{:S(2)}, u32[]{:S(2)}) collective-permute-start(bf16[256,1024]{1,0:T(8,128)(2,1)} %dynamic-slice_convert_fusion), channel_id=1, source_target_pairs={{0,8},{8,0},{16,24},{24,16},{1,9},{9,1},{17,25},{25,17},{2,10},{10... | collective-permute-start | bytes 1572872 | tf_op jit(solution)/shard_map/ppermute | solution.py:46
  236.0 44.5 %collective-permute-start.44 = (bf16[256,1024]{1,0:T(8,128)(2,1)}, bf16[256,1024]{1,0:T(8,128)(2,1)}, u32[]{:S(2)}, u32[]{:S(2)}) collective-permute-start(bf16[256,1024]{1,0:T(8,128)(2,1)} %convolution_convert_fusion.14), channel_id=1, source_target_pairs={{0,16},{8,24},{16,0},{24,8},{1,17},{9,25},{17,1},{25,9},{2,18},{10... | collective-permute-start | bytes 1572872 | tf_op jit(solution)/shard_map/ppermute | solution.py:46
  249.6 114.0 %all-to-all-start.3 = ((bf16[8,1024,128]{2,1,0:T(8,128)(2,1)}), bf16[8,1024,128]{2,1,0:T(8,128)(2,1)}, u32[]{:S(2)}, u32[]{:S(2)}) async-start(bf16[8,1024,128]{2,1,0:T(8,128)(2,1)} %bitcast.97), calls=%async_computation.3 | async-start | bytes 4194304 | tf_op jit(solution)/shard_map/all_to_all | solution.py:40
  275.6 36.8 %collective-permute-start.33 = (bf16[256,1024]{1,0:T(8,128)(2,1)}, bf16[256,1024]{1,0:T(8,128)(2,1)}, u32[]{:S(2)}, u32[]{:S(2)}) collective-permute-start(bf16[256,1024]{1,0:T(8,128)(2,1)} %dynamic-slice_convert_fusion.1), channel_id=1, source_target_pairs={{0,16},{8,24},{16,0},{24,8},{1,17},{9,25},{17,1},{25,9},{2,18},{10... | collective-permute-start | bytes 1572872 | tf_op jit(solution)/shard_map/ppermute | solution.py:46
  276.1 70.8 %collective-permute-start.29 = (bf16[256,1024]{1,0:T(8,128)(2,1)}, bf16[256,1024]{1,0:T(8,128)(2,1)}, u32[]{:S(2)}, u32[]{:S(2)}) collective-permute-start(bf16[256,1024]{1,0:T(8,128)(2,1)} %dynamic-slice_convert_fusion.2), channel_id=1, source_target_pairs={{0,8},{8,0},{16,24},{24,16},{1,9},{9,1},{17,25},{25,17},{2,10},{10... | collective-permute-start | bytes 1572872 | tf_op jit(solution)/shard_map/ppermute | solution.py:46
  280.6 68.9 %collective-permute-start.25 = (bf16[256,1024]{1,0:T(8,128)(2,1)S(1)}, bf16[256,1024]{1,0:T(8,128)(2,1)S(1)}, u32[]{:S(2)}, u32[]{:S(2)}) collective-permute-start(bf16[256,1024]{1,0:T(8,128)(2,1)S(1)} %dynamic-slice_convert_fusion.3), channel_id=1, source_target_pairs={{0,16},{8,24},{16,0},{24,8},{1,17},{9,25},{17,1},{25,9},{2,18},{10... | collective-permute-start | bytes 1572872 | tf_op jit(solution)/shard_map/ppermute | solution.py:46
  303.9 84.4 %collective-permute-start.8 = (bf16[128,4096]{1,0:T(8,128)(2,1)}, bf16[128,4096]{1,0:T(8,128)(2,1)S(1)}, u32[]{:S(2)}, u32[]{:S(2)}) collective-permute-start(bf16[128,4096]{1,0:T(8,128)(2,1)} %convolution_convert_fusion.3), channel_id=1, source_target_pairs={{0,8},{8,0},{16,24},{24,16},{1,9},{9,1},{17,25},{25,17},{2,10},{10... | collective-permute-start | bytes 3145736 | tf_op jit(solution)/shard_map/ppermute | solution.py:46
  318.7 75.4 %collective-permute-start.12 = (bf16[128,4096]{1,0:T(8,128)(2,1)}, bf16[128,4096]{1,0:T(8,128)(2,1)}, u32[]{:S(2)}, u32[]{:S(2)}) collective-permute-start(bf16[128,4096]{1,0:T(8,128)(2,1)} %convolution_convert_fusion.2), channel_id=1, source_target_pairs={{0,16},{8,24},{16,0},{24,8},{1,17},{9,25},{17,1},{25,9},{2,18},{10... | collective-permute-start | bytes 3145736 | tf_op jit(solution)/shard_map/ppermute | solution.py:46
  357.6 39.8 %collective-permute-start.20 = (bf16[128,4096]{1,0:T(8,128)(2,1)}, bf16[128,4096]{1,0:T(8,128)(2,1)}, u32[]{:S(2)}, u32[]{:S(2)}) collective-permute-start(bf16[128,4096]{1,0:T(8,128)(2,1)} %convolution_convert_fusion), channel_id=1, source_target_pairs={{0,16},{8,24},{16,0},{24,8},{1,17},{9,25},{17,1},{25,9},{2,18},{10... | collective-permute-start | bytes 3145736 | tf_op jit(solution)/shard_map/ppermute | solution.py:46
  366.9 63.6 %collective-permute-start = (bf16[256,1024]{1,0:T(8,128)(2,1)}, bf16[256,1024]{1,0:T(8,128)(2,1)}, u32[]{:S(2)}, u32[]{:S(2)}) collective-permute-start(bf16[256,1024]{1,0:T(8,128)(2,1)} %convolution_convert_fusion.17), channel_id=1, source_target_pairs={{0,8},{8,0},{16,24},{24,16},{1,9},{9,1},{17,25},{25,17},{2,10},{10... | collective-permute-start | bytes 1572872 | tf_op jit(solution)/shard_map/ppermute | solution.py:46
  384.4 49.3 %collective-permute-start.4 = (bf16[256,1024]{1,0:T(8,128)(2,1)}, bf16[256,1024]{1,0:T(8,128)(2,1)}, u32[]{:S(2)}, u32[]{:S(2)}) collective-permute-start(bf16[256,1024]{1,0:T(8,128)(2,1)} %convolution_convert_fusion.16), channel_id=1, source_target_pairs={{0,16},{8,24},{16,0},{24,8},{1,17},{9,25},{17,1},{25,9},{2,18},{10... | collective-permute-start | bytes 1572872 | tf_op jit(solution)/shard_map/ppermute | solution.py:46
  453.7 56.9 %collective-permute-start.22 = (bf16[64,4096]{1,0:T(8,128)(2,1)S(1)}, bf16[64,4096]{1,0:T(8,128)(2,1)S(1)}, u32[]{:S(2)}, u32[]{:S(2)}) collective-permute-start(bf16[64,4096]{1,0:T(8,128)(2,1)S(1)} %add_convert_fusion.4), channel_id=1, source_target_pairs={{0,8},{8,0},{16,24},{24,16},{1,9},{9,1},{17,25},{25,17},{2,10},{10... | collective-permute-start | bytes 1572872 | tf_op jit(solution)/shard_map/ppermute | solution.py:46
  454.2 54.6 %collective-permute-start.18 = (bf16[64,4096]{1,0:T(8,128)(2,1)S(1)}, bf16[64,4096]{1,0:T(8,128)(2,1)S(1)}, u32[]{:S(2)}, u32[]{:S(2)}) collective-permute-start(bf16[64,4096]{1,0:T(8,128)(2,1)S(1)} %add_convert_fusion.5), channel_id=1, source_target_pairs={{0,16},{8,24},{16,0},{24,8},{1,17},{9,25},{17,1},{25,9},{2,18},{10... | collective-permute-start | bytes 1572872 | tf_op jit(solution)/shard_map/ppermute | solution.py:46
  460.5 52.2 %collective-permute-start.27 = (bf16[512,1024]{1,0:T(8,128)(2,1)S(1)}, bf16[512,1024]{1,0:T(8,128)(2,1)S(1)}, u32[]{:S(2)}, u32[]{:S(2)}) collective-permute-start(bf16[512,1024]{1,0:T(8,128)(2,1)S(1)} %pad_maximum_fusion.6), channel_id=1, source_target_pairs={{0,8},{8,0},{16,24},{24,16},{1,9},{9,1},{17,25},{25,17},{2,10},{10... | collective-permute-start | bytes 3145736 | tf_op jit(solution)/shard_map/ppermute | solution.py:46
  510.6 35.0 %collective-permute-start.3 = (bf16[256,1024]{1,0:T(8,128)(2,1)S(1)}, bf16[256,1024]{1,0:T(8,128)(2,1)S(1)}, u32[]{:S(2)}, u32[]{:S(2)}) collective-permute-start(bf16[256,1024]{1,0:T(8,128)(2,1)S(1)} %pad_maximum_fusion.10), channel_id=1, source_target_pairs={{0,8},{8,0},{16,24},{24,16},{1,9},{9,1},{17,25},{25,17},{2,10},{10... | collective-permute-start | bytes 1572872 | tf_op jit(solution)/shard_map/ppermute | solution.py:46
  514.1 54.2 %collective-permute-start.15 = (bf16[128,4096]{1,0:T(8,128)(2,1)S(1)}, bf16[128,4096]{1,0:T(8,128)(2,1)S(1)}, u32[]{:S(2)}, u32[]{:S(2)}) collective-permute-start(bf16[128,4096]{1,0:T(8,128)(2,1)S(1)} %pad_maximum_fusion.3), channel_id=1, source_target_pairs={{0,16},{8,24},{16,0},{24,8},{1,17},{9,25},{17,1},{25,9},{2,18},{10... | collective-permute-start | bytes 3145736 | tf_op jit(solution)/shard_map/ppermute | solution.py:46
  534.4 45.1 %collective-permute-start.23 = (bf16[128,4096]{1,0:T(8,128)(2,1)S(1)}, bf16[128,4096]{1,0:T(8,128)(2,1)S(1)}, u32[]{:S(2)}, u32[]{:S(2)}) collective-permute-start(bf16[128,4096]{1,0:T(8,128)(2,1)S(1)} %pad_maximum_fusion.5), channel_id=1, source_target_pairs={{0,16},{8,24},{16,0},{24,8},{1,17},{9,25},{17,1},{25,9},{2,18},{10... | collective-permute-start | bytes 3145736 | tf_op jit(solution)/shard_map/ppermute | solution.py:46
  (77 other events, 980.5 us)
